TPU v7x, 256 devices: a whole 4x4x8 slice. The times are simulated.
256 devices in a mesh: row: 16 (over y_lo, z), col: 16 (over y_hi, x, core).
Axes of the slice: x: 4, y: 4 (y_hi: 2, y_lo: 2; y = y_hi * 2 + y_lo), z: 8, core: 2. Of those that a mesh axis runs over, the one named last changes fastest.
Arguments:
- node_features: bfloat16 [16, 16, 256, 256], P('col', 'row'), may hold values from -6 to 6
- tile_values: bfloat16 [16, 16, 192, 128, 128], P('row', 'col'), may hold values from -0.078125 to 0.078125
- tile_rows: int32 [16, 16, 192], replicated, may hold values from 0 to 31, as said below
- tile_cols: int32 [16, 16, 192], replicated, may hold values from 0 to 31, as said below
- tile_count: int32 [16, 16], replicated, may hold values from 48 to 192, as said below
- weight: bfloat16 [256, 256], replicated, may hold values from -0.375 to 0.375
- cotangent: bfloat16 [16, 16, 256, 256], P('row', 'col'), may hold values from -6 to 6
Outputs:
- activations: bfloat16 [16, 16, 256, 256], P('row', 'col')
- feature_grad: bfloat16 [16, 16, 256, 256], P('col', 'row')
- weight_grad: float32 [256, 256], replicated
Inputs may be any that keep to these rules, and one draw needn't show every extreme that they name: tile_count is 192 on the block whose row group and column group share nodes, and between 48 and 96 on every other block. `tile_rows`: within one device block the slots name distinct (tile row, tile column) pairs. `tile_cols`: within one device block the slots name distinct (tile row, tile column) pairs.
All inputs are finite; a program needn't handle non-finite values.
Results may differ from a plain program's by a relative error of at most 0.023.
Values may be sent and summed in bfloat16 or wider, within the bound.
A program may use at most 128 MiB of HBM per device.

v0:
```python
import math

import jax
import jax.numpy as jnp
from jax import lax
from jax.sharding import PartitionSpec as P


def accumulate(carried, tiles, table, source, target, last_slot, flip):
    slot_total = tiles.shape[0]
    block_width = min(32, slot_total)
    live_span = jnp.maximum(last_slot, 0)
    block_total = (live_span + block_width - 1) // block_width
    lane_ids = jnp.arange(block_width, dtype=jnp.int32)
    pattern = "kba,kbf->kaf" if flip else "kab,kbf->kaf"

    def advance(block_index, running):
        begin_at = block_index * block_width
        start_at = jnp.minimum(begin_at, slot_total - block_width)
        tile_block = lax.dynamic_slice_in_dim(tiles, start_at, block_width, 0)
        picked = lax.dynamic_slice_in_dim(source, start_at, block_width, 0)
        places = lax.dynamic_slice_in_dim(target, start_at, block_width, 0)
        slot_ids = start_at + lane_ids
        usable = (slot_ids >= begin_at) & (slot_ids < last_slot)
        operand = table[picked]
        product = jnp.einsum(pattern, tile_block, operand, preferred_element_type=jnp.float32)
        places = jnp.where(usable, places, running.shape[0])
        return running.at[places].add(product, mode="drop")

    return lax.fori_loop(0, block_total, advance, carried)


def per_device(node_features, tile_values, tile_rows, tile_cols, tile_count, weight, cotangent):
    rows_dev = node_features.shape[2]
    feats = node_features.shape[3]
    edge = tile_values.shape[3]
    n_row = lax.axis_size("row")
    n_col = lax.axis_size("col")
    row_tiles = rows_dev * n_col // edge
    col_tiles = rows_dev * n_row // edge
    my_row = lax.axis_index("row")
    my_col = lax.axis_index("col")
    own_rows = tile_rows[my_row, my_col]
    own_cols = tile_cols[my_row, my_col]
    own_count = tile_count[my_row, my_col]
    tiles = tile_values[0, 0]
    gathered = lax.all_gather(node_features, "row", axis=1, tiled=True)
    feature_table = gathered.reshape(col_tiles, edge, feats)
    partial_value = jnp.zeros((row_tiles, edge, feats), jnp.float32)
    partial_value = accumulate(
        partial_value, tiles, feature_table, own_cols, own_rows, own_count, False
    )
    partial_value = partial_value.reshape(row_tiles * edge, feats)
    contract_rows = (((0,), (0,)), ((), ()))
    summed = lax.psum_scatter(partial_value, "col", scatter_dimension=0, tiled=True)
    aggregated = summed.astype(jnp.bfloat16)
    pre_act = jnp.dot(aggregated, weight, preferred_element_type=jnp.float32)
    logistic = jax.nn.sigmoid(pre_act)
    upstream = cotangent[0, 0].astype(jnp.float32)
    d_pre = (upstream * logistic * (1.0 + pre_act * (1.0 - logistic))).astype(jnp.bfloat16)
    activations = jax.nn.silu(pre_act).astype(jnp.bfloat16)
    weight_part = lax.dot_general(
        aggregated, d_pre, contract_rows, preferred_element_type=jnp.float32
    )
    grad_own = jnp.dot(d_pre, weight.T, preferred_element_type=jnp.float32).astype(jnp.bfloat16)
    grad_group = lax.all_gather(grad_own, "col", axis=0, tiled=True)
    weight_grad = lax.psum(weight_part, ("row", "col")) * (
        1.0 / math.sqrt(rows_dev * n_row * n_col)
    )
    grad_table = grad_group.reshape(row_tiles, edge, feats)
    backward = jnp.zeros((col_tiles, edge, feats), jnp.float32)
    backward = accumulate(backward, tiles, grad_table, own_rows, own_cols, own_count, True)
    feature_grad = lax.psum_scatter(
        backward.reshape(col_tiles * edge, feats).astype(jnp.bfloat16),
        "row",
        scatter_dimension=0,
        tiled=True,
    )
    return (
        activations.reshape(1, 1, rows_dev, feats),
        feature_grad.reshape(1, 1, rows_dev, feats),
        weight_grad,
    )


def solution(mesh):
    in_specs = (
        P("col", "row", None, None),
        P("row", "col", None, None, None),
        P(),
        P(),
        P(),
        P(),
        P("row", "col", None, None),
    )
    out_specs = (P("row", "col", None, None), P("col", "row", None, None), P())
    return jax.shard_map(
        per_device, mesh=mesh, in_specs=in_specs, out_specs=out_specs, check_vma=False
    )
```

profile of v0, /device:TPU:1, one launch (start us, length us, event | category | flops | bytes accessed | tf_op | source)
XLA Modules:
  0.0 655.6 jit_solution(926262493222991625)
XLA Ops:
  10.6 64.9 %all-gather.3.cloned.1.call-done = bf16[1,16,256,256]{3,2,0,1:T(8,128)(2,1)} async-done(((bf16[1,1,256,256]{3,2,0,1:T(8,128)(2,1)}), bf16[1,16,256,256]{3,2,0,1:T(8,128)(2,1)}) %all-gather.3.cloned.1.call-update) | async-done | bytes 2097168 | tf_op jit(solution)/shard_map/all_gather | solution.py:47
  75.5 2.5 broadcast.15.clone
  78.0 50.0 %while.22 = (s32[]{:T(128)}, f32[32,128,256]{2,1,0:T(8,128)}, s32[]{:T(128)}, s32[]{:T(128)}, s32[192]{0:T(256)S(1)}, /*index=5*/bf16[192,128,128]{2,1,0:T(8,128...) while((s32[]{:T(128)}, f32[32,128,256]{2,1,0:T(8,128)}, ...), condition=%wide.region_2.3_spmd.clone, body=%wide.region_0.2_spmd.clone.sunk | while | flops 269485408 | bytes 24122444 | solution.py:30
  80.9 3.9 fusion.33
  84.8 9.9 %scatter_fusion = f32[32,128,256]{2,1,0:T(8,128)} fusion(f32[32,128,256]{2,1,0:T(8,128)} %get-tuple-element.317, s32[32]{0:T(128)S(1)} %get-tuple-element.291, f32[32,128,256]{2,1,0:T(8,128)} %fusion.33), kind=kCustom, calls=%fused_computation.2.clone.clone.1 | custom fusion | flops 1048576 | bytes 12583040 | tf_op jit(solution)/shard_map/while/body/scatter-add | solution.py:28
  97.7 3.9 fusion.33
  101.6 9.9 %scatter_fusion = f32[32,128,256]{2,1,0:T(8,128)} fusion(f32[32,128,256]{2,1,0:T(8,128)} %get-tuple-element.317, s32[32]{0:T(128)S(1)} %get-tuple-element.291, f32[32,128,256]{2,1,0:T(8,128)} %fusion.33), kind=kCustom, calls=%fused_computation.2.clone.clone.1 | custom fusion | flops 1048576 | bytes 12583040 | tf_op jit(solution)/shard_map/while/body/scatter-add | solution.py:28
  114.4 3.9 fusion.33
  118.3 9.7 %scatter_fusion = f32[32,128,256]{2,1,0:T(8,128)} fusion(f32[32,128,256]{2,1,0:T(8,128)} %get-tuple-element.317, s32[32]{0:T(128)S(1)} %get-tuple-element.291, f32[32,128,256]{2,1,0:T(8,128)} %fusion.33), kind=kCustom, calls=%fused_computation.2.clone.clone.1 | custom fusion | flops 1048576 | bytes 12583040 | tf_op jit(solution)/shard_map/while/body/scatter-add | solution.py:28
  128.0 142.7 %reduce-scatter.3.cloned.1.call-done = f32[256,256]{1,0:T(8,128)} async-done(((f32[4096,256]{1,0:T(8,128)}), f32[256,256]{1,0:T(8,128)}) %reduce-scatter.3.cloned.1.call-update) | async-done | bytes 262160 | tf_op jit(solution)/shard_map/reduce_scatter | solution.py:55
  273.6 8.7 %copy.12 = bf16[1,1,192,128,128]{3,4,2,1,0:T(8,128)(2,1)} copy(bf16[1,1,192,128,128]{4,3,2,1,0:T(8,128)(2,1)} %bitcast.30) | data formatting | bytes 12582912 | tf_op args[1]
  283.3 45.5 %all-gather.5.cloned.1.call-done = bf16[4096,256]{1,0:T(8,128)(2,1)} async-done(((bf16[256,256]{1,0:T(8,128)(2,1)}), bf16[4096,256]{1,0:T(8,128)(2,1)}) %all-gather.5.cloned.1.call-update) | async-done | bytes 2097168 | tf_op jit(solution)/shard_map/all_gather | solution.py:66
  328.8 2.5 broadcast.15
  331.3 50.8 %while.23 = (s32[]{:T(128)}, f32[32,128,256]{2,1,0:T(8,128)}, s32[]{:T(128)}, s32[]{:T(128)}, s32[192]{0:T(256)S(1)}, /*index=5*/bf16[192,128,128]{1,2,0:T(8,128...) while((s32[]{:T(128)}, f32[32,128,256]{2,1,0:T(8,128)}, ...), condition=%wide.region_6.7_spmd.clone, body=%wide.region_4.6_spmd.clone.sunk | while | flops 269485408 | bytes 24122444 | solution.py:30
  334.2 4.0 fusion.36
  338.2 9.8 %scatter_fusion.1 = f32[32,128,256]{2,1,0:T(8,128)} fusion(f32[32,128,256]{2,1,0:T(8,128)} %get-tuple-element.356, s32[32]{0:T(128)S(1)} %get-tuple-element.301, f32[32,128,256]{2,1,0:T(8,128)} %fusion.36), kind=kCustom, calls=%fused_computation.3.clone.clone.1 | custom fusion | flops 1048576 | bytes 12583040 | tf_op jit(solution)/shard_map/while/body/scatter-add | solution.py:28
  348.7 2.3 gather_fusion.1
  351.0 4.0 fusion.36
  355.0 10.1 %scatter_fusion.1 = f32[32,128,256]{2,1,0:T(8,128)} fusion(f32[32,128,256]{2,1,0:T(8,128)} %get-tuple-element.356, s32[32]{0:T(128)S(1)} %get-tuple-element.301, f32[32,128,256]{2,1,0:T(8,128)} %fusion.36), kind=kCustom, calls=%fused_computation.3.clone.clone.1 | custom fusion | flops 1048576 | bytes 12583040 | tf_op jit(solution)/shard_map/while/body/scatter-add | solution.py:28
  368.0 4.0 fusion.36
  372.0 10.1 %scatter_fusion.1 = f32[32,128,256]{2,1,0:T(8,128)} fusion(f32[32,128,256]{2,1,0:T(8,128)} %get-tuple-element.356, s32[32]{0:T(128)S(1)} %get-tuple-element.301, f32[32,128,256]{2,1,0:T(8,128)} %fusion.36), kind=kCustom, calls=%fused_computation.3.clone.clone.1 | custom fusion | flops 1048576 | bytes 12583040 | tf_op jit(solution)/shard_map/while/body/scatter-add | solution.py:28
  382.1 3.8 convert_element_type.30
  386.0 197.0 %all-reduce.2.cloned.1.call-done = f32[256,256]{1,0:T(8,128)} async-done(((f32[256,256]{1,0:T(8,128)}), f32[256,256]{1,0:T(8,128)}) %all-reduce.2.cloned.1.call-update) | async-done | bytes 262160 | tf_op jit(solution)/shard_map/psum | solution.py:67
  584.6 64.5 %reduce-scatter.5.cloned.1.call-done = bf16[256,256]{1,0:T(8,128)(2,1)} async-done(((bf16[4096,256]{1,0:T(8,128)(2,1)}), bf16[256,256]{1,0:T(8,128)(2,1)}) %reduce-scatter.5.cloned.1.call-update) | async-done | bytes 131088 | tf_op jit(solution)/shard_map/reduce_scatter | solution.py:73
  (39 shorter events, 23.7 us)
Async XLA Ops:
  7.2 263.6 %copy-start = (bf16[256,256]{1,0:T(8,128)(2,1)S(1)}, bf16[256,256]{1,0:T(8,128)(2,1)}, u32[]{:S(2)}) copy-start(bf16[256,256]{1,0:T(8,128)(2,1)} %param.16) | copy-start | bytes 393220
  7.2 68.3 %all-gather.3.cloned.1.call-start = ((), (), s32[]{:S(2)}) async-start(), calls=%async_computation.2 | async-start | bytes 2228224 | tf_op jit(solution)/shard_map/all_gather | solution.py:47
  7.9 262.9 %reduce-scatter.3.cloned.1.call-start = ((), (), s32[]{:S(2)}) async-start(), calls=%async_computation.3 | async-start | bytes 4456448 | tf_op jit(solution)/shard_map/reduce_scatter | solution.py:55
  127.9 142.8 %copy-start.2 = (bf16[1,1,256,256]{3,2,1,0:T(8,128)(2,1)S(1)}, bf16[1,1,256,256]{3,2,1,0:T(8,128)(2,1)}, u32[]{:S(2)}) copy-start(bf16[1,1,256,256]{3,2,1,0:T(8,128)(2,1)} %param.17) | copy-start | bytes 393220
  128.0 200.8 %all-gather.5.cloned.1.call-start = ((), (), s32[]{:S(2)}) async-start(), calls=%async_computation.4 | async-start | bytes 2228224 | tf_op jit(solution)/shard_map/all_gather | solution.py:66
  273.6 309.4 %all-reduce.2.cloned.1.call-start = ((), (), s32[]{:S(2)}) async-start(), calls=%async_computation.6 | async-start | bytes 524288 | tf_op jit(solution)/shard_map/psum | solution.py:67
  273.6 8.7 %copy-start.1 = (f32[256,256]{1,0:T(8,128)S(1)}, f32[256,256]{1,0:T(8,128)}, u32[]{:S(2)}) copy-start(f32[256,256]{1,0:T(8,128)} %reduce-scatter.3.cloned.1.call-done) | copy-start | bytes 786436
  283.2 365.8 %reduce-scatter.5.cloned.1.call-start = ((), (), s32[]{:S(2)}) async-start(), calls=%async_computation.5 | async-start | bytes 2228224 | tf_op jit(solution)/shard_map/reduce_scatter | solution.py:73
Sparse Core Ops, SparseCore 0:
  9.8 65.6 all-gather.2
  128.1 142.6 reduce-scatter.2
  274.5 54.2 all-gather.4
  335.5 247.3 all-reduce.1
  586.1 62.9 reduce-scatter.4
where the time goes:
time: 668 us; the launch traced here: 656 us
  waiting for transfers between devices  515 us (77%)
  other arithmetic  69 us (10%)
  local copies, waits for them, and re-layouts  29.3 us (4%)
  matrix products  27.3 us (4%)
  between operations  14.4 us (2%)
    psum x1, waiting for transfers between devices, per_device(): lax.psum(weight_part, ('row', 'col'))  197 us
    reduce_scatter x1, waiting for transfers between devices, per_device(): lax.psum_scatter(partial_value, 'col', scatter_dimension=0, tiled=True)  143 us
    all_gather x1, waiting for transfers between devices, per_device(): gathered = lax.all_gather(node_features, 'row', axis=1, tiled=True)  64.9 us
    reduce_scatter x1, waiting for transfers between devices, per_device(): lax.psum_scatter(backward.reshape(col_tiles * edge, feats).astype(jnp.bfl...  64.5 us
    scatter-add x6, other arithmetic, advance(): return running.at[places].add(product, mode='drop')  59.5 us
    all_gather x1, waiting for transfers between devices, per_device(): grad_group = lax.all_gather(grad_own, 'col', axis=0, tiled=True)  45.5 us
    dot_general x6, matrix products, advance(): jnp.einsum(pattern, tile_block, operand, preferred_element_type=jnp.float32)  23.6 us
    gather x6, local copies, waits for them, and re-layouts, advance(): operand = table[picked]  13.7 us
  transfers between devices with their start and end apart: 5, of which 5 were waited for; matrix products, arithmetic and copies ran while one was open for 11% of the time, Pallas kernels for 0%

commit v1 on v0

v1 whole, which is shorter than its diff:
```python
import functools
import math

import jax
import jax.numpy as jnp
from jax import lax
from jax.experimental import pallas as pl
from jax.experimental.pallas import tpu as pltpu
from jax.sharding import PartitionSpec as P

MESH = pl.DeviceIdType.MESH
F32 = jnp.float32
BF16 = jnp.bfloat16

NZ = 8
NX = 4


class Sender:
    def __init__(self, send_sem, recv_sem):
        self.send_sem = send_sem
        self.recv_sem = recv_sem
        self.ids = {}
        self.sent = []

    def slot(self, key):
        if key not in self.ids:
            self.ids[key] = len(self.ids)
        return self.ids[key]

    def copy(self, key, src, dst, device_id):
        n = self.slot(key)
        return pltpu.make_async_remote_copy(
            src_ref=src,
            dst_ref=dst,
            send_sem=self.send_sem.at[n],
            recv_sem=self.recv_sem.at[n],
            device_id=device_id,
            device_id_type=MESH,
        )

    def send(self, key, src, dst, device_id):
        c = self.copy(key, src, dst, device_id)
        c.start()
        self.sent.append(c)

    def wait(self, key, dst, device_id):
        self.copy(key, dst, dst, device_id).wait_recv()

    def finish(self):
        for c in self.sent:
            c.wait_send()
        self.sent = []


def greet(peers):
    barrier = pltpu.get_barrier_semaphore()
    for peer in peers:
        pl.semaphore_signal(barrier, inc=1, device_id=peer, device_id_type=MESH)
    pl.semaphore_wait(barrier, len(peers))


class RowPlace:
    def __init__(self):
        me = lax.axis_index("row")
        self.yl = me // NZ
        self.z = lax.rem(me, NZ)
        self.right = {"row": self.at(self.yl, 1)}
        self.left = {"row": self.at(self.yl, NZ - 1)}
        self.across = {"row": self.at(1 - self.yl, 0)}
        self.peers = [self.right, self.left, self.across]

    def at(self, yl, hops):
        return yl * NZ + lax.rem(self.z + hops + NZ, NZ)


class ColPlace:
    def __init__(self):
        me = lax.axis_index("col")
        self.yh = me // (2 * NX)
        self.x = lax.rem(me // 2, NX)
        self.core = lax.rem(me, 2)
        self.right = {"col": self.at(self.yh, 1, self.core)}
        self.left = {"col": self.at(self.yh, NX - 1, self.core)}
        self.across = {"col": self.at(1 - self.yh, 0, self.core)}
        self.sibling = {"col": self.at(self.yh, 0, 1 - self.core)}
        self.peers = [self.right, self.left, self.across, self.sibling]

    def xat(self, hops):
        return lax.rem(self.x + hops + NX, NX)

    def at(self, yh, hops, core):
        return (yh * NX + self.xat(hops)) * 2 + core


def gather_row_kernel(own_ref, tab, send_sem, recv_sem, local_sem):
    rows = own_ref.shape[0]
    cut = (rows * 7 // 16) // 16 * 16
    half = rows // 2
    cut_half = (cut * 4 // 7) // 16 * 16
    p = RowPlace()
    me = p.at(p.yl, 0)
    local = pltpu.make_async_copy(own_ref, tab.at[me], local_sem)
    local.start()
    s = Sender(send_sem, recv_sem)
    greet(p.peers)

    def part(yl, hops, lo, hi):
        return tab.at[p.at(yl, hops), pl.ds(lo, hi - lo)]

    mine, other = p.yl, 1 - p.yl
    s.send("ya", own_ref.at[pl.ds(0, cut)], part(mine, 0, 0, cut), p.across)
    s.send(("o", 1, 1), own_ref, tab.at[me], p.right)
    s.send(("o", -1, 1), own_ref, tab.at[me], p.left)
    s.send(("yb", 0), own_ref.at[pl.ds(cut, rows - cut)], part(mine, 0, cut, rows), p.across)
    s.wait("ya", part(other, 0, 0, cut), p.across)
    for d, to in ((1, p.right), (-1, p.left)):
        s.send(("a", d, 1), part(other, 0, 0, cut), part(other, 0, 0, cut), to)

    last_own = {1: (0, half), -1: (half, rows)}
    last_cut = {1: (0, cut_half), -1: (cut_half, cut)}
    for h in range(1, NZ // 2 + 1):
        last = h == NZ // 2
        for d, to in ((1, p.right), (-1, p.left)):
            lo, hi = last_own[d] if last else (0, rows)
            s.wait(("o", d, h), part(mine, -d * h, lo, hi), to)
            if not last:
                lo, hi = last_own[d] if h == NZ // 2 - 1 else (0, rows)
                block = part(mine, -d * h, lo, hi)
                s.send(("o", d, h + 1), block, block, to)
                block = part(mine, -d * h, cut, rows)
                s.send(("yb", -d * h), block, block, p.across)
        if last:
            block = part(mine, h, cut, rows)
            s.send(("yb", h), block, block, p.across)
        for d, to in ((1, p.right), (-1, p.left)):
            lo, hi = last_cut[d] if last else (0, cut)
            s.wait(("a", d, h), part(other, -d * h, lo, hi), to)
            if not last:
                lo, hi = last_cut[d] if h == NZ // 2 - 1 else (0, cut)
                block = part(other, -d * h, lo, hi)
                s.send(("a", d, h + 1), block, block, to)
    for k in (0, 1, -1, 2, -2, 3, -3, NZ // 2):
        s.wait(("yb", k), part(other, k, cut, rows), p.across)
    local.wait()
    s.finish()


def gather_row(own):
    rows, feats = own.shape
    n_row = lax.axis_size("row")
    return pl.pallas_call(
        gather_row_kernel,
        out_shape=jax.ShapeDtypeStruct((n_row, rows, feats), own.dtype),
        in_specs=[pl.BlockSpec(memory_space=pltpu.VMEM)],
        out_specs=pl.BlockSpec(memory_space=pltpu.VMEM),
        scratch_shapes=[
            pltpu.SemaphoreType.DMA((40,)),
            pltpu.SemaphoreType.DMA((40,)),
            pltpu.SemaphoreType.DMA,
        ],
        compiler_params=pltpu.CompilerParams(
            collective_id=1, has_side_effects=True, vmem_limit_bytes=32 << 20
        ),
        name="gather_row",
    )(own)


CHUNK = 16
GROUP = 4


def sparse_kernel(flip, tr_ref, tc_ref, cnt_ref, tiles_ref, tab_ref, out_ref, tr, tc, cnt, tiles, acc, sems, isems):
    slots = tiles_ref.shape[0]
    mr, mc = lax.axis_index("row"), lax.axis_index("col")
    ints = [
        pltpu.make_async_copy(tr_ref.at[mr], tr, isems.at[0]),
        pltpu.make_async_copy(tc_ref.at[mr], tc, isems.at[1]),
        pltpu.make_async_copy(cnt_ref, cnt, isems.at[2]),
    ]
    for c in ints:
        c.start()

    def fetch(c):
        piece = pl.ds(c * CHUNK, CHUNK)
        return pltpu.make_async_copy(tiles_ref.at[piece], tiles.at[piece], sems.at[c])

    for c in range(slots // CHUNK):
        fetch(c).start()
    acc[...] = jnp.zeros_like(acc)
    for c in ints:
        c.wait()
    live = cnt[mr, mc]

    def chunk(c, _):
        fetch(c).wait()

        def group(g, _):
            for u in range(GROUP):
                k = c * CHUNK + g * GROUP + u
                r, q = tr[mc, k], tc[mc, k]
                if flip:
                    prod = lax.dot_general(
                        tiles[k], tab_ref[r], (((0,), (0,)), ((), ())), preferred_element_type=F32
                    )
                    to = q
                else:
                    prod = jnp.dot(tiles[k], tab_ref[q], preferred_element_type=F32)
                    to = r
                acc[to] += jnp.where(k < live, prod, 0.0)
            return 0

        left = jnp.clip(live - c * CHUNK, 0, CHUNK)
        lax.fori_loop(0, (left + GROUP - 1) // GROUP, group, 0)
        return 0

    lax.fori_loop(0, slots // CHUNK, chunk, 0)
    out_ref[...] = acc[...].astype(out_ref.dtype)


def sparse(flip, tile_rows, tile_cols, tile_count, tiles, table):
    slots, edge, _ = tiles.shape
    n_tiles, _, feats = table.shape
    n_row, n_col, _ = tile_rows.shape
    hbm = pl.BlockSpec(memory_space=pl.ANY)
    vmem = pl.BlockSpec(memory_space=pltpu.VMEM)
    return pl.pallas_call(
        functools.partial(sparse_kernel, flip),
        out_shape=jax.ShapeDtypeStruct((n_tiles, edge, feats), BF16),
        in_specs=[hbm, hbm, hbm, hbm, vmem],
        out_specs=vmem,
        scratch_shapes=[
            pltpu.SMEM((n_col, slots), jnp.int32),
            pltpu.SMEM((n_col, slots), jnp.int32),
            pltpu.SMEM((n_row, n_col), jnp.int32),
            pltpu.VMEM((slots, edge, edge), BF16),
            pltpu.VMEM((n_tiles, edge, feats), F32),
            pltpu.SemaphoreType.DMA((slots // CHUNK,)),
            pltpu.SemaphoreType.DMA((3,)),
        ],
        compiler_params=pltpu.CompilerParams(vmem_limit_bytes=48 << 20),
        name="sparse_back" if flip else "sparse_forward",
    )(tile_rows, tile_cols, tile_count, tiles, table)


def add_into(dst, src):
    dst[...] = (dst[...].astype(F32) + src[...].astype(F32)).astype(dst.dtype)


def reduce_col(s, p, tag, part, cbuf, xbuf, ybuf, lo, hi):
    half = (hi - lo) // 2
    n = hi - lo
    rows = pl.ds(lo, n)
    sib = 1 - p.core
    for h in (2, 1, 3, 0):
        x = p.xat(h)
        s.send((tag, "c", h), part.at[:, x, sib, rows], cbuf.at[:, x, rows], p.sibling)
    yield

    def take(h):
        x = p.xat(h)
        s.wait((tag, "c", h), cbuf.at[:, x, rows], p.sibling)
        add_into(part.at[:, x, p.core, rows], cbuf.at[:, x, rows])

    way = {1: (p.right, pl.ds(lo, half)), -1: (p.left, pl.ds(lo + half, n - half))}
    take(2)
    for d in (1, -1):
        to, piece = way[d]
        s.send((tag, "x2", d), part.at[:, p.xat(2), p.core, piece], xbuf.at[0, :, piece], to)
    take(1)
    take(3)
    yield
    for d in (1, -1):
        to, piece = way[d]
        x = p.xat(d)
        s.wait((tag, "x2", d), xbuf.at[0, :, piece], to)
        add_into(part.at[:, x, p.core, piece], xbuf.at[0, :, piece])
        slot = 1 if d == 1 else 2
        s.send((tag, "x1", d), part.at[:, x, p.core, rows], xbuf.at[slot, :, rows], to)
    take(0)
    yield
    for d in (1, -1):
        slot = 1 if d == 1 else 2
        s.wait((tag, "x1", d), xbuf.at[slot, :, rows], way[d][0])
    total = part.at[:, p.x, p.core, rows]
    total[...] = (
        total[...].astype(F32) + xbuf[1, :, rows].astype(F32) + xbuf[2, :, rows].astype(F32)
    ).astype(total.dtype)
    s.send((tag, "y"), part.at[1 - p.yh, p.x, p.core, rows], ybuf.at[rows], p.across)
    yield
    s.wait((tag, "y"), ybuf.at[rows], p.across)
    add_into(part.at[p.yh, p.x, p.core, rows], ybuf.at[rows])


def gather_col(s, p, tag, tab, lo, hi):
    n = hi - lo
    half = n // 2
    rows = pl.ds(lo, n)
    mine, other = p.yh, 1 - p.yh
    way = {1: (p.right, pl.ds(lo, half)), -1: (p.left, pl.ds(lo + half, n - half))}

    def block(yh, h, piece):
        return tab.at[yh, p.xat(h), p.core, piece]

    def push(key, b, to):
        s.send((tag,) + key, b, b, to)

    push(("y",), block(mine, 0, rows), p.across)
    for d in (1, -1):
        push(("o", d), block(mine, 0, rows), way[d][0])
    push(("c", 0, 0), block(mine, 0, rows), p.sibling)
    yield
    s.wait((tag, "y"), block(other, 0, rows), p.across)
    for d in (1, -1):
        push(("t", d), block(other, 0, rows), way[d][0])
    push(("c", 1, 0), block(other, 0, rows), p.sibling)
    yield
    for d in (1, -1):
        to, piece = way[d]
        s.wait((tag, "o", d), block(mine, -d, rows), to)
        push(("o2", d), block(mine, -d, piece), to)
        push(("c", 0, -d), block(mine, -d, rows), p.sibling)
    for d in (1, -1):
        to, piece = way[d]
        s.wait((tag, "t", d), block(other, -d, rows), to)
        push(("t2", d), block(other, -d, piece), to)
        push(("c", 1, -d), block(other, -d, rows), p.sibling)
    yield
    for k, (key, yh) in enumerate((("o2", mine), ("t2", other))):
        for d in (1, -1):
            to, piece = way[d]
            s.wait((tag, key, d), block(yh, -2 * d, piece), to)
        push(("c", k, 2), block(yh, 2, rows), p.sibling)
    yield
    for k, yh in ((0, mine), (1, other)):
        for h in (0, -1, 1, 2):
            s.wait((tag, "c", k, h), tab.at[yh, p.xat(h), 1 - p.core, rows], p.sibling)


def drain(*steps):
    steps = list(steps)
    while steps:
        for g in list(steps):
            try:
                next(g)
            except StopIteration:
                steps.remove(g)


def middle_kernel(
    part_ref, w_ref, g_ref, act_ref, etab, wg_ref, part, cbuf, xbuf, ybuf, wpart, wcbuf, wxbuf, wybuf, zbuf,
    send_sem, recv_sem, part_sems,
):
    rows = g_ref.shape[0]
    p = ColPlace()
    q = RowPlace()
    loads = []
    order = [(core, h) for h in (2, 1, 3, 0) for core in (1, 0)]
    for n, (c, h) in enumerate(order):
        core = 1 - p.core if c else p.core
        x = p.xat(h)
        loads.append(pltpu.make_async_copy(part_ref.at[:, x, core], part.at[:, x, core], part_sems.at[n]))
    for c in loads:
        c.start()
    s = Sender(send_sem, recv_sem)
    far = [{"row": q.at(q.yl, h)} for h in (2, 4, 6)]
    greet(p.peers + q.peers + far)
    for c in loads:
        c.wait()
    pieces = 2
    step = rows // pieces
    drain(*[
        reduce_col(s, p, ("r", i), part, cbuf, xbuf, ybuf, i * step, (i + 1) * step) for i in range(pieces)
    ])
    agg = part[p.yh, p.x, p.core]
    pre = jnp.dot(agg, w_ref[...], preferred_element_type=F32)
    logistic = jax.nn.sigmoid(pre)
    upstream = g_ref[...].astype(F32)
    d_pre = (upstream * logistic * (1.0 + pre * (1.0 - logistic))).astype(BF16)
    grad = lax.dot_general(d_pre, w_ref[...], (((1,), (1,)), ((), ())), preferred_element_type=F32)
    etab[p.yh, p.x, p.core] = grad.astype(BF16)

    gathers = [gather_col(s, p, ("g", i), etab, i * step, (i + 1) * step) for i in range(pieces)]
    for g in gathers:
        next(g)

    def weight_sum():
        act_ref[...] = (pre * logistic).astype(act_ref.dtype)
        wg = lax.dot_general(agg, d_pre, (((0,), (0,)), ((), ())), preferred_element_type=F32)
        wpart[...] = wg.reshape(wpart.shape)
        n = wpart.shape[3]
        yield from reduce_col(s, p, "w", wpart, wcbuf, wxbuf, wybuf, 0, n)
        zbuf[0] = wpart[p.yh, p.x, p.core]
        flip = [p_ for p_ in (q.across,)]
        for bit in (1, 2, 4):
            up = lax.rem(q.z // bit, 2)
            z = q.z + bit * (1 - 2 * up)
            flip.append({"row": q.yl * NZ + z})
        for n_, to in enumerate(flip):
            s.send(("wz", n_), zbuf.at[2 * n_], zbuf.at[2 * n_ + 1], to)
            yield
            s.wait(("wz", n_), zbuf.at[2 * n_ + 1], to)
            zbuf[2 * n_ + 2] = zbuf[2 * n_] + zbuf[2 * n_ + 1]

    drain(*gathers, weight_sum())
    wg_ref[...] = zbuf[8]
    s.finish()


def middle(part, weight, cot):
    n_yh, n_x, n_core, rows, feats = part.shape
    n_w = weight.shape[0] // (n_yh * n_x * n_core)
    hbm = pl.BlockSpec(memory_space=pl.ANY)
    vmem = pl.BlockSpec(memory_space=pltpu.VMEM)
    return pl.pallas_call(
        middle_kernel,
        out_shape=(
            jax.ShapeDtypeStruct((rows, feats), BF16),
            jax.ShapeDtypeStruct(part.shape, BF16),
            jax.ShapeDtypeStruct((n_w, feats), F32),
        ),
        in_specs=[hbm, vmem, vmem],
        out_specs=(vmem, vmem, vmem),
        scratch_shapes=[
            pltpu.VMEM(part.shape, BF16),
            pltpu.VMEM((n_yh, n_x, rows, feats), BF16),
            pltpu.VMEM((3, n_yh, rows, feats), BF16),
            pltpu.VMEM((rows, feats), BF16),
            pltpu.VMEM((n_yh, n_x, n_core, n_w, feats), F32),
            pltpu.VMEM((n_yh, n_x, n_w, feats), F32),
            pltpu.VMEM((3, n_yh, n_w, feats), F32),
            pltpu.VMEM((n_w, feats), F32),
            pltpu.VMEM((9, n_w, feats), F32),
            pltpu.SemaphoreType.DMA((100,)),
            pltpu.SemaphoreType.DMA((100,)),
            pltpu.SemaphoreType.DMA((8,)),
        ],
        compiler_params=pltpu.CompilerParams(
            collective_id=2, has_side_effects=True, vmem_limit_bytes=48 << 20
        ),
        name="middle",
    )(part, weight, cot)


def reduce_row(s, p, part, ybuf, obuf, abuf, fbuf):
    rows = part.shape[1]
    cut = (rows * 7 // 16) // 16 * 16
    half = rows // 2
    cut_half = (cut * 4 // 7) // 16 * 16
    mine, other = p.yl, 1 - p.yl
    ways = ((1, p.right), (-1, p.left))
    last_own = {1: (0, half), -1: (half, rows)}
    last_cut = {1: (0, cut_half), -1: (cut_half, cut)}
    top = NZ // 2

    def blk(yl, hops, lo, hi):
        return part.at[p.at(yl, hops), pl.ds(lo, hi - lo)]

    for d, to in ways:
        lo, hi = last_cut[d]
        s.send(("a", d, top), blk(other, top, lo, hi), abuf.at[(top - 1) * 2 + int(d == 1), pl.ds(lo, hi - lo)], to)
    for k in (4, 3, -3, 2, -2, 1, -1, 0):
        s.send(("yb", k), blk(other, k, cut, rows), ybuf.at[k + 3], p.across)
    yield

    def crossed(k):
        s.wait(("yb", k), ybuf.at[k + 3], p.across)
        add_into(blk(mine, k, cut, rows), ybuf.at[k + 3])

    crossed(top)
    for d, to in ways:
        lo, hi = last_own[d]
        s.send(("o", d, top), blk(mine, top, lo, hi), obuf.at[(top - 1) * 2 + int(d == 1), pl.ds(lo, hi - lo)], to)
    for h in range(top - 1, 0, -1):
        yield
        for d, to in ways:
            lo, hi = last_cut[d] if h == top - 1 else (0, cut)
            got = abuf.at[h * 2 + int(d == 1), pl.ds(lo, hi - lo)]
            s.wait(("a", d, h + 1), got, to)
            add_into(blk(other, d * h, lo, hi), got)
            s.send(
                ("a", d, h), blk(other, d * h, 0, cut), abuf.at[(h - 1) * 2 + int(d == 1), pl.ds(0, cut)], to
            )
        for d, to in ways:
            crossed(d * h)
            lo, hi = last_own[d] if h == top - 1 else (0, rows)
            got = obuf.at[h * 2 + int(d == 1), pl.ds(lo, hi - lo)]
            s.wait(("o", d, h + 1), got, to)
            add_into(blk(mine, d * h, lo, hi), got)
            s.send(("o", d, h), blk(mine, d * h, 0, rows), obuf.at[(h - 1) * 2 + int(d == 1)], to)
    crossed(0)
    yield
    for d, to in ways:
        s.wait(("a", d, 1), abuf.at[int(d == 1), pl.ds(0, cut)], to)
    send = blk(other, 0, 0, cut)
    send[...] = (
        send[...].astype(F32) + abuf[0, pl.ds(0, cut)].astype(F32) + abuf[1, pl.ds(0, cut)].astype(F32)
    ).astype(BF16)
    s.send("fin", send, fbuf, p.across)
    for d, to in ways:
        s.wait(("o", d, 1), obuf.at[int(d == 1)], to)
    yield
    s.wait("fin", fbuf, p.across)


def last_kernel(part_ref, wg_ref, out_ref, wout_ref, part, ybuf, obuf, abuf, fbuf, send_sem, recv_sem, part_sems):
    rows, feats = out_ref.shape
    cut = fbuf.shape[0]
    p = RowPlace()
    c = ColPlace()
    loads = []
    order = [(yl, h) for h in (4, 3, -3, 2, -2, 1, -1, 0) for yl in (1, 0)]
    for n, (o, h) in enumerate(order):
        b = p.at(1 - p.yl if o else p.yl, h)
        loads.append(pltpu.make_async_copy(part_ref.at[b], part.at[b], part_sems.at[n]))
    for x in loads:
        x.start()
    s = Sender(send_sem, recv_sem)
    wout_ref[c.yh, c.x, c.core] = wg_ref[...]
    greet(p.peers + c.peers)
    for x in loads:
        x.wait()
    drain(
        reduce_row(s, p, part, ybuf, obuf, abuf, fbuf),
        gather_col(s, c, "w", wout_ref, 0, wg_ref.shape[0]),
    )
    me = p.at(p.yl, 0)
    total = part[me].astype(F32) + obuf[0].astype(F32) + obuf[1].astype(F32)
    out_ref[pl.ds(0, cut)] = (total[:cut] + fbuf[...].astype(F32)).astype(out_ref.dtype)
    out_ref[pl.ds(cut, rows - cut)] = total[cut:].astype(out_ref.dtype)
    s.finish()


def last(part, wg, shape5):
    n_row, rows, feats = part.shape
    cut = (rows * 7 // 16) // 16 * 16
    hbm = pl.BlockSpec(memory_space=pl.ANY)
    vmem = pl.BlockSpec(memory_space=pltpu.VMEM)
    n_yh, n_x, n_core = shape5
    return pl.pallas_call(
        last_kernel,
        out_shape=(
            jax.ShapeDtypeStruct((rows, feats), BF16),
            jax.ShapeDtypeStruct((n_yh, n_x, n_core) + wg.shape, F32),
        ),
        in_specs=[hbm, vmem],
        out_specs=(vmem, vmem),
        scratch_shapes=[
            pltpu.VMEM(part.shape, BF16),
            pltpu.VMEM((NZ, rows - cut, feats), BF16),
            pltpu.VMEM((NZ, rows, feats), BF16),
            pltpu.VMEM((NZ, cut, feats), BF16),
            pltpu.VMEM((cut, feats), BF16),
            pltpu.SemaphoreType.DMA((60,)),
            pltpu.SemaphoreType.DMA((60,)),
            pltpu.SemaphoreType.DMA((16,)),
        ],
        compiler_params=pltpu.CompilerParams(
            collective_id=3, has_side_effects=True, vmem_limit_bytes=48 << 20
        ),
        name="last",
    )(part, wg)


def per_device(node_features, tile_values, tile_rows, tile_cols, tile_count, weight, cotangent):
    rows, feats = node_features.shape[2:]
    edge = tile_values.shape[3]
    n_row = lax.axis_size("row")
    n_col = lax.axis_size("col")
    shape5 = (n_col // (2 * NX), NX, 2)
    tiles = tile_values[0, 0]
    table = gather_row(node_features[0, 0])
    table = table.reshape(n_row * rows // edge, edge, feats)
    part = sparse(False, tile_rows, tile_cols, tile_count, tiles, table)
    part = part.reshape(shape5 + (rows, feats))
    act, etab, wg = middle(part, weight, cotangent[0, 0])
    etab = etab.reshape(n_col * rows // edge, edge, feats)
    back = sparse(True, tile_rows, tile_cols, tile_count, tiles, etab)
    grad, wgrad = last(back.reshape(n_row, rows, feats), wg, shape5)
    wgrad = wgrad.reshape(feats, feats) * (1.0 / math.sqrt(rows * n_row * n_col))
    return act[None, None], grad[None, None], wgrad


def solution(mesh):
    in_specs = (
        P("col", "row", None, None),
        P("row", "col", None, None, None),
        P(),
        P(),
        P(),
        P(),
        P("row", "col", None, None),
    )
    out_specs = (P("row", "col", None, None), P("col", "row", None, None), P())
    return jax.shard_map(
        per_device, mesh=mesh, in_specs=in_specs, out_specs=out_specs, check_vma=False
    )
```

time: 668 us -> 150 us (0.22); the launches traced: 656 us -> 149 us
  waiting for transfers between devices: 515 us -> 0 us
  Pallas kernels: 0 us -> 145 us
  other arithmetic: 69 us -> 0.73 us
  matrix products: 27.3 us -> 0 us
  local copies, waits for them, and re-layouts: 29.3 us -> 2.29 us
  between operations: 14.4 us -> 0.75 us
    reduce_scatter x2 -> x0, waiting for transfers between devices: 207 us -> none  [the longest x1 143 us: per_device(): lax.psum_scatter(partial_value, 'col', scatter_dimension=0, tiled=True)]
    psum x1 -> x0, waiting for transfers between devices: 197 us -> none  [per_device(): lax.psum(weight_part, ('row', 'col'))]
    pallas_call x0 -> x5, Pallas kernels: none -> 145 us  [the longest x1 60.3 us: middle(): pl.pallas_call(middle_kernel, out_shape=(jax.ShapeDtypeStruct((rows, feat...]
    all_gather x2 -> x0, waiting for transfers between devices: 110 us -> none  [the longest x1 64.9 us: per_device(): gathered = lax.all_gather(node_features, 'row', axis=1, tiled=True)]
    scatter-add x6 -> x0, other arithmetic: 59.5 us -> none  [advance(): return running.at[places].add(product, mode='drop')]
    dot_general x9 -> x0, matrix products: 27.3 us -> none  [the longest x6 23.6 us: advance(): jnp.einsum(pattern, tile_block, operand, preferred_element_type=jnp.float32)]
    gather x6 -> x0, local copies, waits for them, and re-layouts: 13.7 us -> none  [advance(): operand = table[picked]]
  transfers between devices with their start and end apart: 5 -> 0, of which waited for: 5 -> 0; matrix products, arithmetic and copies ran while one was open for 11% -> 0% of each run, Pallas kernels for 0% -> 0%
where the time goes in v1:
time: 150 us; the launch traced here: 149 us
  Pallas kernels  145 us (97%)
  local copies, waits for them, and re-layouts  2.29 us (2%)
    pallas_call x1, Pallas kernels, middle(): pl.pallas_call(middle_kernel, out_shape=(jax.ShapeDtypeStruct((rows, feat...  60.3 us
    pallas_call x1, Pallas kernels, last(): pl.pallas_call(last_kernel, out_shape=(jax.ShapeDtypeStruct((rows, feats)...  48.1 us
    pallas_call x1, Pallas kernels, gather_row(): pl.pallas_call(gather_row_kernel, out_shape=jax.ShapeDtypeStruct((n_row,...  26.2 us
    pallas_call x2, Pallas kernels, sparse(): pl.pallas_call(functools.partial(sparse_kernel, flip), out_shape=jax.Shap...  10.5 us

profile of v1, /device:TPU:1, one launch (start us, length us, event | category | flops | bytes accessed | tf_op | source)
XLA Modules:
  0.0 148.9 jit_solution(1912326583753140062)
XLA Ops:
  0.6 0.0 copy-start.1
  0.6 0.0 copy-start
  0.7 0.0 copy-start.2
  0.7 1.0 copy-done.2
  1.6 0.0 copy-start.5
  1.6 26.2 %gather_row.1 = bf16[16,256,256]{2,1,0:T(8,128)(2,1)S(1)} custom-call(bf16[256,256]{1,0:T(8,128)(2,1)S(1)} %bitcast.14), custom_call_target="tpu_custom_call" | custom-call | tf_op jit(solution)/shard_map/gather_row/pallas_call | solution.py:152
  27.8 0.0 copy-done.1
  27.8 0.0 copy-done
  27.8 0.0 copy-done.5
  27.8 0.0 copy-start.3
  27.8 0.0 copy-start.4
  27.8 5.0 %sparse_forward.1 = bf16[32,128,256]{2,1,0:T(8,128)(2,1)S(1)} custom-call(s32[16,16,192]{2,1,0:T(8,128)S(1)} %copy-done, s32[16,16,192]{2,1,0:T(8,128)S(1)} %copy-done.1, s32[16,16]{1,0:T(8,128)S(1)} %copy-done.5, bf16[192,128,128]{2,1,0:T(8,128)(2,1)} %bitcast.18, bf16[32,128,256]{2,1,0:T(8,128)(2,1)S(1)} %bitcast.12), custom_call_target="tpu_custom_call" | custom-call | tf_op jit(solution)/shard_map/sparse_forward/pallas_call | solution.py:227
  32.9 0.0 copy-done.3
  32.9 0.0 copy-done.4
  32.9 60.3 %middle.1 = (bf16[256,256]{1,0:T(8,128)(2,1)S(1)}, bf16[2,4,2,256,256]{4,3,2,1,0:T(8,128)(2,1)S(1)}, f32[16,256]{1,0:T(8,128)S(1)}) custom-call(bf16[2,4,2,256,256]{4,3,2,1,0:T(8,128)(2,1)S(1)} %bitcast.10, bf16[256,256]{1,0:T(8,128)(2,1)S(1)} %copy-done.3, bf16[256,256]{1,0:T(8,128)(2,1)S(1)} %bitcast.15), custom_call_target="tpu_custom_call" | custom-call | tf_op jit(solution)/shard_map/middle/pallas_call | solution.py:415
  93.2 5.5 %sparse_back.1 = bf16[32,128,256]{2,1,0:T(8,128)(2,1)S(1)} custom-call(s32[16,16,192]{2,1,0:T(8,128)S(1)} %copy-done, s32[16,16,192]{2,1,0:T(8,128)S(1)} %copy-done.1, s32[16,16]{1,0:T(8,128)S(1)} %copy-done.5, bf16[192,128,128]{2,1,0:T(8,128)(2,1)} %bitcast.19, bf16[32,128,256]{2,1,0:T(8,128)(2,1)S(1)} %bitcast.13), custom_call_target="tpu_custom_call" | custom-call | tf_op jit(solution)/shard_map/sparse_back/pallas_call | solution.py:227
  98.7 48.1 %last.1 = (bf16[256,256]{1,0:T(8,128)(2,1)S(1)}, f32[2,4,2,16,256]{4,3,2,1,0:T(8,128)S(1)}) custom-call(bf16[16,256,256]{2,1,0:T(8,128)(2,1)S(1)} %bitcast.11, f32[16,256]{1,0:T(8,128)S(1)} %get-tuple-element.10.wg_ref), custom_call_target="tpu_custom_call" | custom-call | tf_op jit(solution)/shard_map/last/pallas_call | solution.py:540
  146.9 0.7 broadcast_multiply_fusion
  147.6 0.7 copy.12
  148.2 0.7 copy.13
Async XLA Ops:
  0.6 27.1 %copy-start.1 = (s32[16,16,192]{2,1,0:T(8,128)S(1)}, s32[16,16,192]{2,1,0:T(8,128)}, u32[]{:S(2)}) copy-start(s32[16,16,192]{2,1,0:T(8,128)} %tc_ref.3) | copy-start | bytes 589828
  0.6 27.1 %copy-start = (s32[16,16,192]{2,1,0:T(8,128)S(1)}, s32[16,16,192]{2,1,0:T(8,128)}, u32[]{:S(2)}) copy-start(s32[16,16,192]{2,1,0:T(8,128)} %tr_ref.3) | copy-start | bytes 589828
  0.7 1.0 copy-start.2
  1.6 26.2 %copy-start.5 = (s32[16,16]{1,0:T(8,128)S(1)}, s32[16,16]{1,0:T(8,128)}, u32[]{:S(2)}) copy-start(s32[16,16]{1,0:T(8,128)} %cnt_ref.3) | copy-start | bytes 3076
  27.8 5.1 %copy-start.3 = (bf16[256,256]{1,0:T(8,128)(2,1)S(1)}, bf16[256,256]{1,0:T(8,128)(2,1)}, u32[]{:S(2)}) copy-start(bf16[256,256]{1,0:T(8,128)(2,1)} %w_ref.1) | copy-start | bytes 393220
  27.8 5.1 %copy-start.4 = (bf16[1,1,256,256]{3,2,1,0:T(8,128)(2,1)S(1)}, bf16[1,1,256,256]{3,2,1,0:T(8,128)(2,1)}, u32[]{:S(2)}) copy-start(bf16[1,1,256,256]{3,2,1,0:T(8,128)(2,1)} %param.13) | copy-start | bytes 393220

commit v2 on v1

v2 whole, which is shorter than its diff:
```python
import functools
import math

import jax
import jax.numpy as jnp
from jax import lax
from jax.experimental import pallas as pl
from jax.experimental.pallas import tpu as pltpu
from jax.sharding import PartitionSpec as P

MESH = pl.DeviceIdType.MESH
F32 = jnp.float32
BF16 = jnp.bfloat16

NZ = 8
NX = 4
TILE = 128
PLACES = 256


class Sender:
    def __init__(self, send_sem, recv_sem):
        self.send_sem = send_sem
        self.recv_sem = recv_sem
        self.ids = {}
        self.sent = []

    def slot(self, key):
        if key not in self.ids:
            self.ids[key] = len(self.ids)
        return self.ids[key]

    def copy(self, key, src, dst, device_id):
        n = self.slot(key)
        return pltpu.make_async_remote_copy(
            src_ref=src,
            dst_ref=dst,
            send_sem=self.send_sem.at[n],
            recv_sem=self.recv_sem.at[n],
            device_id=device_id,
            device_id_type=MESH,
        )

    def send(self, key, src, dst, device_id):
        c = self.copy(key, src, dst, device_id)
        c.start()
        self.sent.append(c)

    def wait(self, key, dst, device_id):
        self.copy(key, dst, dst, device_id).wait_recv()

    def finish(self):
        for c in self.sent:
            c.wait_send()
        self.sent = []


def greet(peers):
    barrier = pltpu.get_barrier_semaphore()
    for peer in peers:
        pl.semaphore_signal(barrier, inc=1, device_id=peer, device_id_type=MESH)
    pl.semaphore_wait(barrier, len(peers))


class RowPlace:
    def __init__(self):
        me = lax.axis_index("row")
        self.yl = me // NZ
        self.z = lax.rem(me, NZ)
        self.right = {"row": self.at(self.yl, 1)}
        self.left = {"row": self.at(self.yl, NZ - 1)}
        self.across = {"row": self.at(1 - self.yl, 0)}
        self.peers = [self.right, self.left, self.across]

    def at(self, yl, hops):
        return yl * NZ + lax.rem(self.z + hops + NZ, NZ)


class ColPlace:
    def __init__(self):
        me = lax.axis_index("col")
        self.yh = me // (2 * NX)
        self.x = lax.rem(me // 2, NX)
        self.core = lax.rem(me, 2)
        self.right = {"col": self.at(self.yh, 1, self.core)}
        self.left = {"col": self.at(self.yh, NX - 1, self.core)}
        self.across = {"col": self.at(1 - self.yh, 0, self.core)}
        self.sibling = {"col": self.at(self.yh, 0, 1 - self.core)}
        self.peers = [self.right, self.left, self.across, self.sibling]
        self.mates = [(dy, h) for dy in (0, 1) for h in range(NX) if (dy, h) != (0, 0)]

    def mate(self, dy, h):
        return {"col": self.at(self.yh + dy - 2 * self.yh * dy, h, self.core)}

    def xat(self, hops):
        return lax.rem(self.x + hops + NX, NX)

    def at(self, yh, hops, core):
        return (yh * NX + self.xat(hops)) * 2 + core


def order_slots(rows, cols, live, n_tiles, plan):
    slots = rows.shape[1]
    places = plan.shape[1]
    steps = (slots + n_tiles) // 2
    sub = lax.broadcasted_iota(jnp.int32, (slots, slots), 0)
    lane = lax.broadcasted_iota(jnp.int32, (slots, slots), 1)
    k_row, k_col = lane[:1].astype(F32), sub[:, :1].astype(F32)
    live_row, live_col = lane[:1] < live, sub[:, :1] < live
    tile = lax.broadcasted_iota(jnp.int32, (n_tiles, slots), 0).astype(F32)
    place = lax.broadcasted_iota(jnp.int32, (slots, places), 1).astype(F32)
    tile_sub = lax.broadcasted_iota(jnp.int32, (n_tiles, places), 0)
    tile_lane = lax.broadcasted_iota(jnp.int32, (n_tiles, places), 1)

    def turn(row):
        return jnp.sum(jnp.where(sub == lane, row, 0.0), axis=1, keepdims=True)

    out = []
    for key, source in ((rows, cols), (cols, rows)):
        key, source = key.astype(F32), source.astype(F32)
        same = (turn(key) == key) & (sub < lane) & live_col
        rank = jnp.sum(jnp.where(same, 1.0, 0.0), axis=0, keepdims=True)
        number = jnp.sum(jnp.where((tile == key) & live_row, 1.0, 0.0), axis=1, keepdims=True)
        pairs = jnp.floor((number + 1.0) * 0.5)
        base = 2.0 * jnp.sum(jnp.where(tile < key, pairs, 0.0), axis=0, keepdims=True)
        at = turn(jnp.where(live_row, base + rank, -1.0))
        hit = at == place
        slot = slots + jnp.sum(jnp.where(hit, k_col - slots, 0.0), axis=0, keepdims=True)
        read = jnp.sum(jnp.where(hit, turn(source), 0.0), axis=0, keepdims=True)
        fresh = jnp.sum(jnp.where(hit & (turn(rank) == 0.0), 1.0, 0.0), axis=0, keepdims=True)
        upto = jnp.sum(jnp.where(tile_sub <= tile_lane, pairs, 0.0), axis=0, keepdims=True)
        some = jnp.sum(jnp.where(tile_sub == tile_lane, number, 0.0), axis=0, keepdims=True)
        final = jnp.where(some > 0.0, upto - 1.0, float(steps))
        out += [slot, read, fresh, final]
    for n, x in enumerate(out):
        plan[pl.ds(n, 1)] = x.astype(jnp.int32)


def gather_row_kernel(tr_ref, tc_ref, cnt_ref, own_ref, tab, plan_ref, tr, tc, cnt, send_sem, recv_sem, local_sem):
    rows = own_ref.shape[0]
    cut = (rows * 7 // 16) // 16 * 16
    half = rows // 2
    cut_half = (cut * 4 // 7) // 16 * 16
    p = RowPlace()
    me = p.at(p.yl, 0)
    mr, mc = lax.axis_index("row"), lax.axis_index("col")
    local = [
        pltpu.make_async_copy(tr_ref.at[mr], tr, local_sem.at[0]),
        pltpu.make_async_copy(tc_ref.at[mr], tc, local_sem.at[1]),
        pltpu.make_async_copy(cnt_ref, cnt, local_sem.at[2]),
        pltpu.make_async_copy(own_ref, tab.at[me], local_sem.at[3]),
    ]
    for c in local:
        c.start()
    s = Sender(send_sem, recv_sem)
    greet(p.peers)

    def part(yl, hops, lo, hi):
        return tab.at[p.at(yl, hops), pl.ds(lo, hi - lo)]

    mine, other = p.yl, 1 - p.yl
    s.send("ya", own_ref.at[pl.ds(0, cut)], part(mine, 0, 0, cut), p.across)
    s.send(("o", 1, 1), own_ref, tab.at[me], p.right)
    s.send(("o", -1, 1), own_ref, tab.at[me], p.left)
    s.send(("yb", 0), own_ref.at[pl.ds(cut, rows - cut)], part(mine, 0, cut, rows), p.across)
    for c in local:
        c.wait()
    order_slots(tr[pl.ds(mc, 1)], tc[pl.ds(mc, 1)], cnt[mr, mc], tab.shape[0] * rows // TILE, plan_ref)
    s.wait("ya", part(other, 0, 0, cut), p.across)
    for d, to in ((1, p.right), (-1, p.left)):
        s.send(("a", d, 1), part(other, 0, 0, cut), part(other, 0, 0, cut), to)

    last_own = {1: (0, half), -1: (half, rows)}
    last_cut = {1: (0, cut_half), -1: (cut_half, cut)}
    for h in range(1, NZ // 2 + 1):
        last = h == NZ // 2
        for d, to in ((1, p.right), (-1, p.left)):
            lo, hi = last_own[d] if last else (0, rows)
            s.wait(("o", d, h), part(mine, -d * h, lo, hi), to)
            if not last:
                lo, hi = last_own[d] if h == NZ // 2 - 1 else (0, rows)
                block = part(mine, -d * h, lo, hi)
                s.send(("o", d, h + 1), block, block, to)
                block = part(mine, -d * h, cut, rows)
                s.send(("yb", -d * h), block, block, p.across)
        if last:
            block = part(mine, h, cut, rows)
            s.send(("yb", h), block, block, p.across)
        for d, to in ((1, p.right), (-1, p.left)):
            lo, hi = last_cut[d] if last else (0, cut)
            s.wait(("a", d, h), part(other, -d * h, lo, hi), to)
            if not last:
                lo, hi = last_cut[d] if h == NZ // 2 - 1 else (0, cut)
                block = part(other, -d * h, lo, hi)
                s.send(("a", d, h + 1), block, block, to)
    for k in (0, 1, -1, 2, -2, 3, -3, NZ // 2):
        s.wait(("yb", k), part(other, k, cut, rows), p.across)
    s.finish()


def gather_row(own, tile_rows, tile_cols, tile_count):
    rows, feats = own.shape
    n_row, n_col, slots = tile_rows.shape
    hbm = pl.BlockSpec(memory_space=pl.ANY)
    vmem = pl.BlockSpec(memory_space=pltpu.VMEM)
    return pl.pallas_call(
        gather_row_kernel,
        out_shape=(
            jax.ShapeDtypeStruct((n_row, rows, feats), own.dtype),
            jax.ShapeDtypeStruct((8, PLACES), jnp.int32),
        ),
        in_specs=[hbm, hbm, hbm, vmem],
        out_specs=(vmem, vmem),
        scratch_shapes=[
            pltpu.VMEM((n_col, slots), jnp.int32),
            pltpu.VMEM((n_col, slots), jnp.int32),
            pltpu.SMEM((n_row, n_col), jnp.int32),
            pltpu.SemaphoreType.DMA((40,)),
            pltpu.SemaphoreType.DMA((40,)),
            pltpu.SemaphoreType.DMA((4,)),
        ],
        compiler_params=pltpu.CompilerParams(
            collective_id=1, has_side_effects=True, vmem_limit_bytes=32 << 20
        ),
        name="gather_row",
    )(tile_rows, tile_cols, tile_count, own)


CHUNK = 16
GROUP = 4


def multiply(flip, plan, tiles, tab, stash, out):
    steps = stash.shape[0] - 1
    first = 4 if flip else 0
    side = (0, 0) if flip else (1, 0)
    shape = stash.shape[1:]

    def some(g, acc):
        for u in range(GROUP):
            p = g * GROUP + u
            k = [plan[first, 2 * p + i] for i in (0, 1)]
            q = [plan[first + 1, 2 * p + i] for i in (0, 1)]
            left = jnp.concatenate([tiles[i] for i in k], axis=side[0])
            right = jnp.concatenate([tab[i] for i in q], axis=0)
            prod = lax.dot_general(left, right, (((side[0],), (0,)), ((), ())), preferred_element_type=F32)
            fresh = plan[first + 2, 2 * p] == 1
            acc = jnp.where(fresh, 0.0, acc) + prod
            stash[p] = acc.astype(stash.dtype)
        return acc

    lax.fori_loop(0, steps // GROUP, some, jnp.zeros(shape, F32))
    stash[steps] = jnp.zeros(shape, stash.dtype)
    for t in range(out.shape[0]):
        out[t] = stash[plan[first + 3, t]]


def sparse_kernel(flip, plan_ref, tiles_ref, tab_ref, out_ref, plan, tiles, stash, sems, psem):
    slots, edge, _ = tiles_ref.shape
    get = pltpu.make_async_copy(plan_ref, plan, psem)
    get.start()
    chunks = []
    for c in range(slots // CHUNK):
        piece = pl.ds(c * CHUNK, CHUNK)
        chunks.append(pltpu.make_async_copy(tiles_ref.at[piece], tiles.at[piece], sems.at[c]))
    for c in chunks:
        c.start()
    tiles[slots] = jnp.zeros((edge, edge), tiles.dtype)
    get.wait()
    for c in chunks:
        c.wait()
    multiply(flip, plan, tiles, tab_ref, stash, out_ref)


def sparse(flip, plan, tiles, table):
    slots, edge, _ = tiles.shape
    n_tiles, _, feats = table.shape
    hbm = pl.BlockSpec(memory_space=pl.ANY)
    vmem = pl.BlockSpec(memory_space=pltpu.VMEM)
    return pl.pallas_call(
        functools.partial(sparse_kernel, flip),
        out_shape=jax.ShapeDtypeStruct((n_tiles, edge, feats), BF16),
        in_specs=[hbm, hbm, vmem],
        out_specs=vmem,
        scratch_shapes=[
            pltpu.SMEM(plan.shape, jnp.int32),
            pltpu.VMEM((slots + 1, edge, edge), BF16),
            pltpu.VMEM(((slots + n_tiles) // 2 + 1, edge, feats), BF16),
            pltpu.SemaphoreType.DMA((slots // CHUNK,)),
            pltpu.SemaphoreType.DMA,
        ],
        compiler_params=pltpu.CompilerParams(vmem_limit_bytes=48 << 20),
        name="sparse_back" if flip else "sparse_forward",
    )(plan, tiles, table)


def add_into(dst, *terms):
    total = dst[...].astype(F32)
    for t in terms:
        total = total + t[...].astype(F32)
    dst[...] = total.astype(dst.dtype)


def reduce_col(s, p, tag, part, cbuf, xa2, xa1, xb2, xb1, yb, ya):
    rows = part.shape[3]
    half = rows // 2
    qr = half // 2
    a_, b_ = pl.ds(0, half), pl.ds(half, half)
    mine, other, core, sib = p.yh, 1 - p.yh, p.core, 1 - p.core
    ways = ((1, p.right, 0), (-1, p.left, 1))

    def cuts(n, base):
        return pl.ds(base + n * qr, qr)

    def both(n, h, ds):
        s.send((tag, "c", n, h), part.at[:, p.xat(h), sib, ds], cbuf.at[:, p.xat(h), ds], p.sibling)

    def one(n, yh, h, ds):
        s.send((tag, "c", n, h), part.at[yh, p.xat(h), sib, ds], cbuf.at[yh, p.xat(h), ds], p.sibling)

    def took_both(n, h, ds):
        got = cbuf.at[:, p.xat(h), ds]
        s.wait((tag, "c", n, h), got, p.sibling)
        return got

    def took_one(n, yh, h, ds):
        got = cbuf.at[yh, p.xat(h), ds]
        s.wait((tag, "c", n, h), got, p.sibling)
        return got

    for h in (2, 1, -1, 0):
        one("o", other, h, b_)
    both("a", 2, a_)
    one("b", mine, 2, b_)
    for h in (1, -1):
        both("a", h, a_)
    for h in (1, -1):
        one("b", mine, h, b_)
    both("a", 0, a_)
    one("b", mine, 0, b_)
    yield
    for h in (2, 1, -1, 0):
        send = part.at[other, p.xat(h), core, b_]
        add_into(send, took_one("o", other, h, b_))
        s.send((tag, "yb", h), send, yb.at[h % NX], p.across)
        if h == 2:
            add_into(part.at[:, p.xat(2), core, a_], took_both("a", 2, a_))
            for d, to, n in ways:
                s.send((tag, "xa2", d), part.at[:, p.xat(2), core, cuts(n, 0)], xa2.at[:, cuts(n, 0)], to)
    add_into(part.at[mine, p.xat(2), core, b_], took_one("b", mine, 2, b_))
    for h in (1, -1):
        add_into(part.at[:, p.xat(h), core, a_], took_both("a", h, a_))
    for h in (1, -1):
        add_into(part.at[mine, p.xat(h), core, b_], took_one("b", mine, h, b_))
    yield
    s.wait((tag, "yb", 2), yb.at[2], p.across)
    add_into(part.at[mine, p.xat(2), core, b_], yb.at[2])
    for d, to, n in ways:
        s.send((tag, "xb2", d), part.at[mine, p.xat(2), core, cuts(n, half)], xb2.at[cuts(n, 0)], to)
    yield
    for d, to, n in ways:
        s.wait((tag, "xa2", d), xa2.at[:, cuts(n, 0)], to)
        add_into(part.at[:, p.xat(d), core, cuts(n, 0)], xa2.at[:, cuts(n, 0)])
        s.send((tag, "xa1", d), part.at[:, p.xat(d), core, a_], xa1.at[n], to)
    add_into(part.at[:, p.x, core, a_], took_both("a", 0, a_))
    add_into(part.at[mine, p.x, core, b_], took_one("b", mine, 0, b_))
    yield
    for d, to, n in ways:
        s.wait((tag, "yb", d), yb.at[d % NX], p.across)
        add_into(part.at[mine, p.xat(d), core, b_], yb.at[d % NX])
        s.wait((tag, "xb2", d), xb2.at[cuts(n, 0)], to)
        add_into(part.at[mine, p.xat(d), core, cuts(n, half)], xb2.at[cuts(n, 0)])
        s.send((tag, "xb1", d), part.at[mine, p.xat(d), core, b_], xb1.at[n], to)
    yield
    for d, to, n in ways:
        s.wait((tag, "xa1", d), xa1.at[n], to)
    add_into(part.at[:, p.x, core, a_], xa1.at[0], xa1.at[1])
    s.send((tag, "ya"), part.at[other, p.x, core, a_], ya, p.across)
    s.wait((tag, "yb", 0), yb.at[0], p.across)
    yield
    for d, to, n in ways:
        s.wait((tag, "xb1", d), xb1.at[n], to)
    add_into(part.at[mine, p.x, core, b_], yb.at[0], xb1.at[0], xb1.at[1])
    yield
    s.wait((tag, "ya"), ya, p.across)
    add_into(part.at[mine, p.x, core, a_], ya)


def reduce_col_scratch(n_yh, n_x, rows, feats):
    half = rows // 2
    return [
        pltpu.VMEM((n_yh, n_x, rows, feats), BF16),
        pltpu.VMEM((n_yh, half, feats), BF16),
        pltpu.VMEM((2, n_yh, half, feats), BF16),
        pltpu.VMEM((half, feats), BF16),
        pltpu.VMEM((2, half, feats), BF16),
        pltpu.VMEM((n_x, half, feats), BF16),
        pltpu.VMEM((half, feats), BF16),
    ]


def gather_col(s, p, tag, tab):
    rows = tab.shape[3]
    half = rows // 2
    qr = half // 2
    a_, b_, all_ = pl.ds(0, half), pl.ds(half, half), pl.ds(0, rows)
    mine, other = p.yh, 1 - p.yh
    ways = ((1, p.right, 0), (-1, p.left, 1))
    sibs = []

    def block(yh, h, ds):
        return tab.at[yh, p.xat(h), p.core, ds]

    def push(key, b, to):
        s.send((tag,) + key, b, b, to)

    def share(k, h, ds, name):
        push(("c", k, h, name), block((mine, other)[k], h, ds), p.sibling)
        sibs.append((k, h, ds, name))

    def took(key, yh, h, ds):
        s.wait((tag,) + key, block(yh, h, ds), p.sibling)

    push(("y",), block(mine, 0, a_), p.across)
    for d, to, n in ways:
        push(("ob", d), block(mine, 0, b_), to)
    for d, to, n in ways:
        push(("oa", d), block(mine, 0, a_), to)
    push(("yb", 0), block(mine, 0, b_), p.across)
    share(0, 0, all_, "f")
    yield
    took(("y",), other, 0, a_)
    for d, to, n in ways:
        push(("ta", d), block(other, 0, a_), to)
    share(1, 0, a_, "a")
    yield
    for d, to, n in ways:
        took(("ob", d), mine, -d, b_)
        push(("ob2", d), block(mine, -d, pl.ds(half + n * qr, qr)), to)
        push(("yb", -d), block(mine, -d, b_), p.across)
        share(0, -d, b_, "b")
    for d, to, n in ways:
        took(("oa", d), mine, -d, a_)
        push(("oa2", d), block(mine, -d, pl.ds(n * qr, qr)), to)
        share(0, -d, a_, "a")
    yield
    for d, to, n in ways:
        took(("ta", d), other, -d, a_)
        push(("ta2", d), block(other, -d, pl.ds(n * qr, qr)), to)
        share(1, -d, a_, "a")
    took(("yb", 0), other, 0, b_)
    share(1, 0, b_, "b")
    yield
    for d, to, n in ways:
        took(("ob2", d), mine, 2, pl.ds(half + n * qr, qr))
    push(("yb", 2), block(mine, 2, b_), p.across)
    share(0, 2, b_, "b")
    yield
    for d in (1, -1):
        took(("yb", d), other, d, b_)
        share(1, d, b_, "b")
    for d, to, n in ways:
        took(("oa2", d), mine, 2, pl.ds(n * qr, qr))
    share(0, 2, a_, "a")
    yield
    for d, to, n in ways:
        took(("ta2", d), other, 2, pl.ds(n * qr, qr))
    share(1, 2, a_, "a")
    took(("yb", 2), other, 2, b_)
    share(1, 2, b_, "b")
    yield
    for k, h, ds, name in sibs:
        s.wait((tag, "c", k, h, name), tab.at[(mine, other)[k], p.xat(h), 1 - p.core, ds], p.sibling)


def drain(*steps):
    steps = list(steps)
    while steps:
        for g in list(steps):
            try:
                next(g)
            except StopIteration:
                steps.remove(g)


def sum_weight(s, p, q, wpart, wc, wd, wy, wz, scale):
    core, sib = p.core, 1 - p.core
    s.send("wc", wpart.at[:, :, sib], wc, p.sibling)
    yield
    s.wait("wc", wc, p.sibling)
    mine = wpart.at[:, :, core]
    mine[...] = mine[...] + wc[...]
    for dy, h in p.mates:
        yh = p.yh + dy - 2 * p.yh * dy
        s.send(("wd", dy, h), wpart.at[yh, p.xat(h), core], wd.at[dy * NX + h], p.mate(dy, h))
    yield
    total = wpart[p.yh, p.x, core]
    for dy, h in p.mates:
        s.wait(("wd", dy, h), wd.at[dy * NX + h], p.mate(dy, h))
        total = total + wd[dy * NX + h]
    wy[0] = total
    s.send("wy", wy.at[0], wy.at[1], q.across)
    yield
    s.wait("wy", wy.at[1], q.across)
    wz[q.z] = wy[0] + wy[1]
    for h in range(1, NZ):
        s.send(("wz", h), wz.at[q.z], wz.at[q.z], {"row": q.at(q.yl, h)})
    yield
    for h in range(1, NZ):
        s.wait(("wz", h), wz.at[lax.rem(q.z - h + NZ, NZ)], q.across)
    total = wz[0]
    for z in range(1, NZ):
        total = total + wz[z]
    wy[2] = total * scale


def middle_kernel(scale, part_ref, w_ref, g_ref, act_ref, etab, wg_ref, part, *rest):
    bufs, (wpart, wc, wd, wy, wz, send_sem, recv_sem, part_sems) = rest[:7], rest[7:]
    p = ColPlace()
    q = RowPlace()
    loads = []
    for n in range(2):
        core = (1 - p.core, p.core)[n]
        loads.append(pltpu.make_async_copy(part_ref.at[:, :, core], part.at[:, :, core], part_sems.at[n]))
    for c in loads:
        c.start()
    s = Sender(send_sem, recv_sem)
    greet(
        [p.sibling, q.across]
        + [p.mate(dy, h) for dy, h in p.mates]
        + [{"row": q.at(q.yl, h)} for h in range(1, NZ)]
    )
    for c in loads:
        c.wait()
    drain(reduce_col(s, p, "r", part, *bufs))
    agg = part[p.yh, p.x, p.core]
    pre = jnp.dot(agg, w_ref[...], preferred_element_type=F32)
    logistic = jax.nn.sigmoid(pre)
    upstream = g_ref[...].astype(F32)
    d_pre = (upstream * logistic * (1.0 + pre * (1.0 - logistic))).astype(BF16)
    grad = lax.dot_general(d_pre, w_ref[...], (((1,), (1,)), ((), ())), preferred_element_type=F32)
    etab[p.yh, p.x, p.core] = grad.astype(BF16)
    gather = gather_col(s, p, "g", etab)
    next(gather)
    act_ref[...] = (pre * logistic).astype(act_ref.dtype)
    wg = lax.dot_general(agg, d_pre, (((0,), (0,)), ((), ())), preferred_element_type=F32)
    wpart[...] = wg.reshape(wpart.shape)
    drain(sum_weight(s, p, q, wpart, wc, wd, wy, wz, scale), gather)
    wg_ref[...] = wy[2]
    s.finish()


def middle(part, weight, cot, scale):
    n_yh, n_x, n_core, rows, feats = part.shape
    n_w = weight.shape[0] // (n_yh * n_x * n_core)
    hbm = pl.BlockSpec(memory_space=pl.ANY)
    vmem = pl.BlockSpec(memory_space=pltpu.VMEM)
    return pl.pallas_call(
        functools.partial(middle_kernel, scale),
        out_shape=(
            jax.ShapeDtypeStruct((rows, feats), BF16),
            jax.ShapeDtypeStruct(part.shape, BF16),
            jax.ShapeDtypeStruct((n_w, feats), F32),
        ),
        in_specs=[hbm, vmem, vmem],
        out_specs=(vmem, vmem, vmem),
        scratch_shapes=[pltpu.VMEM(part.shape, BF16)]
        + reduce_col_scratch(n_yh, n_x, rows, feats)
        + [
            pltpu.VMEM((n_yh, n_x, n_core, n_w, feats), F32),
            pltpu.VMEM((n_yh, n_x, n_w, feats), F32),
            pltpu.VMEM((n_yh * n_x, n_w, feats), F32),
            pltpu.VMEM((3, n_w, feats), F32),
            pltpu.VMEM((NZ, n_w, feats), F32),
            pltpu.SemaphoreType.DMA((100,)),
            pltpu.SemaphoreType.DMA((100,)),
            pltpu.SemaphoreType.DMA((2,)),
        ],
        compiler_params=pltpu.CompilerParams(
            collective_id=2, has_side_effects=True, vmem_limit_bytes=48 << 20
        ),
        name="middle",
    )(part, weight, cot)


def reduce_row(s, p, part, ybuf, obuf, abuf, fbuf):
    rows = part.shape[1]
    cut = (rows * 7 // 16) // 16 * 16
    half = rows // 2
    cut_half = (cut * 4 // 7) // 16 * 16
    mine, other = p.yl, 1 - p.yl
    ways = ((1, p.right), (-1, p.left))
    last_own = {1: (0, half), -1: (half, rows)}
    last_cut = {1: (0, cut_half), -1: (cut_half, cut)}
    top = NZ // 2

    def blk(yl, hops, lo, hi):
        return part.at[p.at(yl, hops), pl.ds(lo, hi - lo)]

    for d, to in ways:
        lo, hi = last_cut[d]
        s.send(("a", d, top), blk(other, top, lo, hi), abuf.at[(top - 1) * 2 + int(d == 1), pl.ds(lo, hi - lo)], to)
    for k in (4, 3, -3, 2, -2, 1, -1, 0):
        s.send(("yb", k), blk(other, k, cut, rows), ybuf.at[k + 3], p.across)
    yield

    def crossed(k):
        s.wait(("yb", k), ybuf.at[k + 3], p.across)
        add_into(blk(mine, k, cut, rows), ybuf.at[k + 3])

    crossed(top)
    for d, to in ways:
        lo, hi = last_own[d]
        s.send(("o", d, top), blk(mine, top, lo, hi), obuf.at[(top - 1) * 2 + int(d == 1), pl.ds(lo, hi - lo)], to)
    for h in range(top - 1, 0, -1):
        yield
        for d, to in ways:
            lo, hi = last_cut[d] if h == top - 1 else (0, cut)
            got = abuf.at[h * 2 + int(d == 1), pl.ds(lo, hi - lo)]
            s.wait(("a", d, h + 1), got, to)
            add_into(blk(other, d * h, lo, hi), got)
            s.send(
                ("a", d, h), blk(other, d * h, 0, cut), abuf.at[(h - 1) * 2 + int(d == 1), pl.ds(0, cut)], to
            )
        for d, to in ways:
            crossed(d * h)
            lo, hi = last_own[d] if h == top - 1 else (0, rows)
            got = obuf.at[h * 2 + int(d == 1), pl.ds(lo, hi - lo)]
            s.wait(("o", d, h + 1), got, to)
            add_into(blk(mine, d * h, lo, hi), got)
            s.send(("o", d, h), blk(mine, d * h, 0, rows), obuf.at[(h - 1) * 2 + int(d == 1)], to)
    crossed(0)
    yield
    for d, to in ways:
        s.wait(("a", d, 1), abuf.at[int(d == 1), pl.ds(0, cut)], to)
    send = blk(other, 0, 0, cut)
    send[...] = (
        send[...].astype(F32) + abuf[0, pl.ds(0, cut)].astype(F32) + abuf[1, pl.ds(0, cut)].astype(F32)
    ).astype(BF16)
    s.send("fin", send, fbuf, p.across)
    for d, to in ways:
        s.wait(("o", d, 1), obuf.at[int(d == 1)], to)
    yield
    s.wait("fin", fbuf, p.across)


def gather_weight(s, p, tab):
    own = tab.at[p.yh, p.x, p.core]
    for dy, h in p.mates:
        s.send(("w", dy, h), own, own, p.mate(dy, h))
    yield
    yield
    yield
    for dy, h in p.mates:
        yh = p.yh + dy - 2 * p.yh * dy
        s.wait(("w", dy, h), tab.at[yh, p.xat(-h), p.core], p.sibling)
    s.send("ws", tab.at[:, :, p.core], tab.at[:, :, p.core], p.sibling)
    yield
    yield
    s.wait("ws", tab.at[:, :, 1 - p.core], p.sibling)


def last_kernel(part_ref, wg_ref, out_ref, wout_ref, part, ybuf, obuf, abuf, fbuf, send_sem, recv_sem, part_sems):
    rows, feats = out_ref.shape
    cut = fbuf.shape[0]
    p = RowPlace()
    c = ColPlace()
    loads = [
        pltpu.make_async_copy(part_ref.at[pl.ds(yl * NZ, NZ)], part.at[pl.ds(yl * NZ, NZ)], part_sems.at[n])
        for n, yl in enumerate((1 - p.yl, p.yl))
    ]
    for x in loads:
        x.start()
    s = Sender(send_sem, recv_sem)
    wout_ref[c.yh, c.x, c.core] = wg_ref[...]
    greet(p.peers + [c.sibling] + [c.mate(dy, h) for dy, h in c.mates])
    for x in loads:
        x.wait()
    drain(
        reduce_row(s, p, part, ybuf, obuf, abuf, fbuf),
        gather_weight(s, c, wout_ref),
    )
    me = p.at(p.yl, 0)
    total = part[me].astype(F32) + obuf[0].astype(F32) + obuf[1].astype(F32)
    out_ref[pl.ds(0, cut)] = (total[:cut] + fbuf[...].astype(F32)).astype(out_ref.dtype)
    out_ref[pl.ds(cut, rows - cut)] = total[cut:].astype(out_ref.dtype)
    s.finish()


def last(part, wg, shape5):
    n_row, rows, feats = part.shape
    cut = (rows * 7 // 16) // 16 * 16
    hbm = pl.BlockSpec(memory_space=pl.ANY)
    vmem = pl.BlockSpec(memory_space=pltpu.VMEM)
    n_yh, n_x, n_core = shape5
    return pl.pallas_call(
        last_kernel,
        out_shape=(
            jax.ShapeDtypeStruct((rows, feats), BF16),
            jax.ShapeDtypeStruct((n_yh, n_x, n_core) + wg.shape, F32),
        ),
        in_specs=[hbm, vmem],
        out_specs=(vmem, vmem),
        scratch_shapes=[
            pltpu.VMEM(part.shape, BF16),
            pltpu.VMEM((NZ, rows - cut, feats), BF16),
            pltpu.VMEM((NZ, rows, feats), BF16),
            pltpu.VMEM((NZ, cut, feats), BF16),
            pltpu.VMEM((cut, feats), BF16),
            pltpu.SemaphoreType.DMA((60,)),
            pltpu.SemaphoreType.DMA((60,)),
            pltpu.SemaphoreType.DMA((2,)),
        ],
        compiler_params=pltpu.CompilerParams(
            collective_id=3, has_side_effects=True, vmem_limit_bytes=48 << 20
        ),
        name="last",
    )(part, wg)


def per_device(node_features, tile_values, tile_rows, tile_cols, tile_count, weight, cotangent):
    rows, feats = node_features.shape[2:]
    edge = tile_values.shape[3]
    n_row = lax.axis_size("row")
    n_col = lax.axis_size("col")
    shape5 = (n_col // (2 * NX), NX, 2)
    tiles = tile_values[0, 0]
    table, plan = gather_row(node_features[0, 0], tile_rows, tile_cols, tile_count)
    table = table.reshape(n_row * rows // edge, edge, feats)
    part = sparse(False, plan, tiles, table)
    part = part.reshape(shape5 + (rows, feats))
    act, etab, wg = middle(part, weight, cotangent[0, 0], 1.0 / math.sqrt(rows * n_row * n_col))
    etab = etab.reshape(n_col * rows // edge, edge, feats)
    back = sparse(True, plan, tiles, etab)
    grad, wgrad = last(back.reshape(n_row, rows, feats), wg, shape5)
    return act[None, None], grad[None, None], wgrad.reshape(feats, feats)


def solution(mesh):
    in_specs = (
        P("col", "row", None, None),
        P("row", "col", None, None, None),
        P(),
        P(),
        P(),
        P(),
        P("row", "col", None, None),
    )
    out_specs = (P("row", "col", None, None), P("col", "row", None, None), P())
    return jax.shard_map(
        per_device, mesh=mesh, in_specs=in_specs, out_specs=out_specs, check_vma=False
    )
```

time: 150 us -> 128 us (0.85)
  Pallas kernels: 145 us -> 121 us
  local copies, waits for them, and re-layouts: 2.29 us -> 5.52 us
    pallas_call x1, Pallas kernels: 48.1 us -> 26.6 us  [last(): pl.pallas_call(last_kernel, out_shape=(jax.ShapeDtypeStruct((rows, feats)...]
    pallas_call x2, Pallas kernels: 86.5 us -> 73.4 us  [the longest x1 47.1 us: middle(): pl.pallas_call(functools.partial(middle_kernel, scale), out_shape=(jax.Sh...]
    pallas_call x2, Pallas kernels: 10.5 us -> 20.5 us  [sparse(): pl.pallas_call(functools.partial(sparse_kernel, flip), out_shape=jax.Shap...]
    unnamed x14 -> x15, local copies, waits for them, and re-layouts: 2.29 us -> 5.52 us
where the time goes in v2:
time: 128 us; the launch traced here: 127 us
  Pallas kernels  121 us (95%)
  local copies, waits for them, and re-layouts  5.52 us (4%)
    pallas_call x1, Pallas kernels, middle(): pl.pallas_call(functools.partial(middle_kernel, scale), out_shape=(jax.Sh...  47.1 us
    pallas_call x1, Pallas kernels, last(): pl.pallas_call(last_kernel, out_shape=(jax.ShapeDtypeStruct((rows, feats)...  26.6 us
    pallas_call x1, Pallas kernels, gather_row(): pl.pallas_call(gather_row_kernel, out_shape=(jax.ShapeDtypeStruct((n_row,...  26.2 us
    pallas_call x2, Pallas kernels, sparse(): pl.pallas_call(functools.partial(sparse_kernel, flip), out_shape=jax.Shap...  20.5 us
    unnamed x15, local copies, waits for them, and re-layouts  5.52 us

profile of v2, /device:TPU:1, one launch (start us, length us, event | category | flops | bytes accessed | tf_op | source)
XLA Modules:
  0.0 126.8 jit_solution(6673366161192416620)
XLA Ops:
  0.6 0.0 copy-start
  0.6 0.9 copy-done
  1.6 0.0 copy-start.1
  1.6 0.9 copy-done.1
  2.5 0.0 copy-start.4
  2.5 0.9 copy-done.4
  3.4 0.0 copy-start.5
  3.4 0.7 copy-done.5
  4.1 26.2 %gather_row.1 = (bf16[16,256,256]{2,1,0:T(8,128)(2,1)S(1)}, s32[8,256]{1,0:T(8,128)S(1)}) custom-call(s32[16,16,192]{2,1,0:T(8,128)S(1)} %copy-done, s32[16,16,192]{2,1,0:T(8,128)S(1)} %copy-done.1, s32[16,16]{1,0:T(8,128)S(1)} %copy-done.5, bf16[256,256]{1,0:T(8,128)(2,1)S(1)} %bitcast.18), custom_call_target="tpu_custom_call" | custom-call | tf_op jit(solution)/shard_map/gather_row/pallas_call | solution.py:206
  30.4 0.0 copy-start.2
  30.4 0.0 copy-start.3
  30.4 9.9 %sparse_forward.1 = bf16[32,128,256]{2,1,0:T(8,128)(2,1)S(1)} custom-call(s32[8,256]{1,0:T(8,128)S(1)} %get-tuple-element.10.plan_ref, bf16[192,128,128]{2,1,0:T(8,128)(2,1)} %bitcast.19, bf16[32,128,256]{2,1,0:T(8,128)(2,1)S(1)} %bitcast.13), custom_call_target="tpu_custom_call" | custom-call | tf_op jit(solution)/shard_map/sparse_forward/pallas_call | solution.py:280
  40.3 0.0 copy-done.2
  40.3 0.0 copy-done.3
  40.3 47.1 %middle.1 = (bf16[256,256]{1,0:T(8,128)(2,1)S(1)}, bf16[2,4,2,256,256]{4,3,2,1,0:T(8,128)(2,1)S(1)}, f32[16,256]{1,0:T(8,128)S(1)}) custom-call(bf16[2,4,2,256,256]{4,3,2,1,0:T(8,128)(2,1)S(1)} %bitcast.11, bf16[256,256]{1,0:T(8,128)(2,1)S(1)} %copy-done.2, bf16[256,256]{1,0:T(8,128)(2,1)S(1)} %bitcast.15), custom_call_target="tpu_custom_call" | custom-call | tf_op jit(solution)/shard_map/middle/pallas_call | solution.py:558
  87.5 10.6 %sparse_back.1 = bf16[32,128,256]{2,1,0:T(8,128)(2,1)S(1)} custom-call(s32[8,256]{1,0:T(8,128)S(1)} %get-tuple-element.10.plan_ref, bf16[192,128,128]{2,1,0:T(8,128)(2,1)} %bitcast.20, bf16[32,128,256]{2,1,0:T(8,128)(2,1)S(1)} %bitcast.12), custom_call_target="tpu_custom_call" | custom-call | tf_op jit(solution)/shard_map/sparse_back/pallas_call | solution.py:280
  98.1 26.6 %last.1 = (bf16[256,256]{1,0:T(8,128)(2,1)S(1)}, f32[2,4,2,16,256]{4,3,2,1,0:T(8,128)S(1)}) custom-call(bf16[16,256,256]{2,1,0:T(8,128)(2,1)S(1)} %bitcast.10, f32[16,256]{1,0:T(8,128)S(1)} %get-tuple-element.14.wg_ref), custom_call_target="tpu_custom_call" | custom-call | tf_op jit(solution)/shard_map/last/pallas_call | solution.py:696
  124.7 0.7 copy.13
  125.4 0.7 copy.14
  126.0 0.7 copy.15
Async XLA Ops:
  0.6 1.0 copy-start
  1.6 0.9 copy-start.1
  2.5 0.9 copy-start.4
  3.4 0.7 copy-start.5
  30.4 9.9 %copy-start.2 = (bf16[256,256]{1,0:T(8,128)(2,1)S(1)}, bf16[256,256]{1,0:T(8,128)(2,1)}, u32[]{:S(2)}) copy-start(bf16[256,256]{1,0:T(8,128)(2,1)} %w_ref.1) | copy-start | bytes 393220
  30.4 9.9 %copy-start.3 = (bf16[1,1,256,256]{3,2,1,0:T(8,128)(2,1)S(1)}, bf16[1,1,256,256]{3,2,1,0:T(8,128)(2,1)}, u32[]{:S(2)}) copy-start(bf16[1,1,256,256]{3,2,1,0:T(8,128)(2,1)} %param.13) | copy-start | bytes 393220

commit v3 on v0

v3 whole, which is shorter than its diff:
```python
import functools
import math

import jax
import jax.numpy as jnp
from jax import lax
from jax.experimental import pallas as pl
from jax.experimental.pallas import tpu as pltpu
from jax.sharding import PartitionSpec as P

MESH = pl.DeviceIdType.MESH
F32 = jnp.float32
BF16 = jnp.bfloat16

NZ = 8
NX = 4
TILE = 128
PLACES = 256


class Sender:
    def __init__(self, send_sem, recv_sem):
        self.send_sem = send_sem
        self.recv_sem = recv_sem
        self.ids = {}
        self.sent = []

    def slot(self, key):
        if key not in self.ids:
            self.ids[key] = len(self.ids)
        return self.ids[key]

    def copy(self, key, src, dst, device_id):
        n = self.slot(key)
        return pltpu.make_async_remote_copy(
            src_ref=src,
            dst_ref=dst,
            send_sem=self.send_sem.at[n],
            recv_sem=self.recv_sem.at[n],
            device_id=device_id,
            device_id_type=MESH,
        )

    def send(self, key, src, dst, device_id):
        c = self.copy(key, src, dst, device_id)
        c.start()
        self.sent.append(c)

    def wait(self, key, dst, device_id):
        self.copy(key, dst, dst, device_id).wait_recv()

    def finish(self):
        for c in self.sent:
            c.wait_send()
        self.sent = []


class RowPlace:
    def __init__(self):
        me = lax.axis_index("row")
        self.yl = me // NZ
        self.z = lax.rem(me, NZ)
        self.right = {"row": self.at(self.yl, 1)}
        self.left = {"row": self.at(self.yl, NZ - 1)}
        self.across = {"row": self.at(1 - self.yl, 0)}

    def zat(self, hops):
        return lax.rem(self.z + hops + NZ, NZ)

    def at(self, yl, hops):
        return yl * NZ + self.zat(hops)


class ColPlace:
    def __init__(self):
        me = lax.axis_index("col")
        self.yh = me // (2 * NX)
        self.x = lax.rem(me // 2, NX)
        self.core = lax.rem(me, 2)
        self.right = {"col": self.at(self.yh, 1, self.core)}
        self.left = {"col": self.at(self.yh, NX - 1, self.core)}
        self.across = {"col": self.at(1 - self.yh, 0, self.core)}
        self.sibling = {"col": self.at(self.yh, 0, 1 - self.core)}
        self.mates = [(dy, h) for dy in (0, 1) for h in range(NX) if (dy, h) != (0, 0)]

    def mate(self, dy, h):
        return {"col": self.at(self.yh + dy - 2 * self.yh * dy, h, self.core)}

    def xat(self, hops):
        return lax.rem(self.x + hops + NX, NX)

    def at(self, yh, hops, core):
        return (yh * NX + self.xat(hops)) * 2 + core


def order_slots(rows, cols, live, n_tiles, plan):
    slots = rows.shape[1]
    places = plan.shape[1]
    steps = (slots + n_tiles) // 2
    sub = lax.broadcasted_iota(jnp.int32, (slots, slots), 0)
    lane = lax.broadcasted_iota(jnp.int32, (slots, slots), 1)
    k_col = sub[:, :1]
    live_row, live_col = lane[:1] < live, sub[:, :1] < live
    tile = lax.broadcasted_iota(jnp.int32, (n_tiles, slots), 0)
    place = lax.broadcasted_iota(jnp.int32, (slots, places), 1)
    tile_sub = lax.broadcasted_iota(jnp.int32, (n_tiles, places), 0)
    tile_lane = lax.broadcasted_iota(jnp.int32, (n_tiles, places), 1)

    def turn(row):
        return jnp.sum(jnp.where(sub == lane, row, 0), axis=1, keepdims=True)

    out = []
    for key, source in ((rows, cols), (cols, rows)):
        same = (turn(key) == key) & (sub < lane) & live_col
        rank = jnp.sum(jnp.where(same, 1, 0), axis=0, keepdims=True)
        number = jnp.sum(jnp.where((tile == key) & live_row, 1, 0), axis=1, keepdims=True)
        pairs = (number + 1) >> 1
        base = 2 * jnp.sum(jnp.where(tile < key, pairs, 0), axis=0, keepdims=True)
        at = turn(jnp.where(live_row, base + rank, -1))
        hit = at == place
        slot = slots + jnp.sum(jnp.where(hit, k_col - slots, 0), axis=0, keepdims=True)
        read = jnp.sum(jnp.where(hit, turn(source), 0), axis=0, keepdims=True)
        fresh = jnp.sum(jnp.where(hit & (turn(rank) == 0), 1, 0), axis=0, keepdims=True)
        upto = jnp.sum(jnp.where(tile_sub <= tile_lane, pairs, 0), axis=0, keepdims=True)
        some = jnp.sum(jnp.where(tile_sub == tile_lane, number, 0), axis=0, keepdims=True)
        final = jnp.where(some > 0, upto - 1, steps)
        out += [slot, read, fresh, final]
    for n, x in enumerate(out):
        plan[pl.ds(n, 1)] = x


GROUP = 16


def multiply(flip, plan, tiles, tab, stash):
    steps = stash.shape[0] - 1
    first = 4 if flip else 0
    side = 0 if flip else 1
    shape = stash.shape[1:]

    def some(g, acc):
        for u in range(GROUP):
            p = g * GROUP + u
            k = [plan[first, 2 * p + i] for i in (0, 1)]
            q = [plan[first + 1, 2 * p + i] for i in (0, 1)]
            left = jnp.concatenate([tiles[i] for i in k], axis=side)
            right = jnp.concatenate([tab[i] for i in q], axis=0)
            prod = lax.dot_general(left, right, (((side,), (0,)), ((), ())), preferred_element_type=F32)
            fresh = plan[first + 2, 2 * p] == 1
            acc = jnp.where(fresh, 0.0, acc) + prod
            stash[p] = acc.astype(stash.dtype)
        return acc

    lax.fori_loop(0, steps // GROUP, some, jnp.zeros(shape, F32))
    stash[steps] = jnp.zeros(shape, stash.dtype)


def add_into(dst, *terms):
    total = dst[...].astype(F32)
    for t in terms:
        total = total + t[...].astype(F32)
    dst[...] = total.astype(dst.dtype)


def cut_of(rows):
    return (rows * 7 // 16) // 16 * 16


def gather_row(s, p, tag, tab):
    rows = tab.shape[2]
    cut = cut_of(rows)
    top = NZ // 2
    mine, other = p.yl, 1 - p.yl
    ways = ((1, p.right), (-1, p.left))
    a_, b_ = pl.ds(0, cut), pl.ds(cut, rows - cut)
    a_last = {1: pl.ds(0, cut // 2 // 16 * 16 + 16), -1: pl.ds(cut // 2 // 16 * 16 + 16, cut - cut // 2 // 16 * 16 - 16)}
    b_half = (rows - cut) // 2 // 16 * 16
    b_last = {1: pl.ds(cut, b_half), -1: pl.ds(cut + b_half, rows - cut - b_half)}

    def blk(yl, h, ds):
        return tab.at[yl, p.zat(h), ds]

    def pair(h, ds):
        return tab.at[:, p.zat(h), ds]

    def push(key, b, to):
        s.send((tag,) + key, b, b, to)

    push(("ya",), blk(mine, 0, a_), p.across)
    for d, to in ways:
        push(("b", d, 1), blk(mine, 0, b_), to)
    push(("yb", 0), blk(mine, 0, b_), p.across)
    yield
    s.wait((tag, "ya"), blk(other, 0, a_), p.across)
    for d, to in ways:
        push(("a", d, 1), pair(0, a_), to)
    for h in range(1, top + 1):
        yield
        for d, to in ways:
            s.wait((tag, "b", d, h), blk(mine, -d * h, b_last[d] if h == top else b_), to)
            if h < top:
                push(("b", d, h + 1), blk(mine, -d * h, b_last[d] if h == top - 1 else b_), to)
                push(("yb", -d * h), blk(mine, -d * h, b_), p.across)
        if h == top:
            push(("yb", top), blk(mine, top, b_), p.across)
        yield
        for d, to in ways:
            s.wait((tag, "a", d, h), pair(-d * h, a_last[d] if h == top else a_), to)
            if h < top:
                push(("a", d, h + 1), pair(-d * h, a_last[d] if h == top - 1 else a_), to)
    yield
    for h in [0] + [d * h for h in range(1, top) for d in (1, -1)] + [top]:
        s.wait((tag, "yb", h), blk(other, h, b_), p.across)


def reduce_row(s, p, tag, part, ybuf, abuf, bbuf, fbuf):
    rows = part.shape[2]
    cut = cut_of(rows)
    top = NZ // 2
    mine, other = p.yl, 1 - p.yl
    ways = ((1, p.right, 0), (-1, p.left, 1))
    a_, b_ = pl.ds(0, cut), pl.ds(cut, rows - cut)
    a_mid = cut // 2 // 16 * 16 + 16
    b_mid = (rows - cut) // 2 // 16 * 16
    a_last = {1: (0, a_mid), -1: (a_mid, cut)}
    b_last = {1: (0, b_mid), -1: (b_mid, rows - cut)}

    def a_cut(d, h):
        lo, hi = a_last[d] if h == top else (0, cut)
        return pl.ds(lo, hi - lo)

    def b_cut(d, h, base=0):
        lo, hi = b_last[d] if h == top else (0, rows - cut)
        return pl.ds(base + lo, hi - lo)

    for h in [top] + [d * h for h in range(top - 1, 0, -1) for d in (1, -1)] + [0]:
        s.send((tag, "yb", h), part.at[other, p.zat(h), b_], ybuf.at[h + top - 1], p.across)
        if h == top:
            for d, to, n in ways:
                ds = a_cut(d, top)
                s.send((tag, "a", d, top), part.at[:, p.zat(top), ds], abuf.at[top - 1, n, :, ds], to)
    for h in range(top, 0, -1):
        yield
        for d, to, n in ways:
            if h < top:
                ds = a_cut(d, h + 1)
                got = abuf.at[h, n, :, ds]
                s.wait((tag, "a", d, h + 1), got, to)
                add_into(part.at[:, p.zat(d * h), ds], got)
                s.send((tag, "a", d, h), part.at[:, p.zat(d * h), a_], abuf.at[h - 1, n], to)
        yield
        for d, to, n in ways:
            if h < top or d == 1:
                s.wait((tag, "yb", d * h), ybuf.at[d * h + top - 1], p.across)
                add_into(part.at[mine, p.zat(d * h), b_], ybuf.at[d * h + top - 1])
            if h < top:
                got = bbuf.at[h, n, b_cut(d, h + 1)]
                s.wait((tag, "b", d, h + 1), got, to)
                add_into(part.at[mine, p.zat(d * h), b_cut(d, h + 1, cut)], got)
            ds = b_cut(d, h)
            s.send((tag, "b", d, h), part.at[mine, p.zat(d * h), b_cut(d, h, cut)], bbuf.at[h - 1, n, ds], to)
    yield
    for d, to, n in ways:
        s.wait((tag, "a", d, 1), abuf.at[0, n], to)
    add_into(part.at[:, p.z, a_], abuf.at[0, 0], abuf.at[0, 1])
    s.send((tag, "f"), part.at[other, p.z, a_], fbuf, p.across)
    s.wait((tag, "yb", 0), ybuf.at[top - 1], p.across)
    yield
    for d, to, n in ways:
        s.wait((tag, "b", d, 1), bbuf.at[0, n], to)
    add_into(part.at[mine, p.z, b_], ybuf.at[top - 1], bbuf.at[0, 0], bbuf.at[0, 1])
    yield
    s.wait((tag, "f"), fbuf, p.across)
    add_into(part.at[mine, p.z, a_], fbuf)


def reduce_row_scratch(rows, feats):
    cut, top = cut_of(rows), NZ // 2
    return [
        pltpu.VMEM((NZ, rows - cut, feats), BF16),
        pltpu.VMEM((top, 2, 2, cut, feats), BF16),
        pltpu.VMEM((top, 2, rows - cut, feats), BF16),
        pltpu.VMEM((cut, feats), BF16),
    ]


def reduce_col(s, p, tag, part, cbuf, xa2, xa1, xb2, xb1, yb, ya):
    rows = part.shape[3]
    half = rows // 2
    qr = half // 2
    a_, b_ = pl.ds(0, half), pl.ds(half, half)
    mine, other, core, sib = p.yh, 1 - p.yh, p.core, 1 - p.core
    ways = ((1, p.right, 0), (-1, p.left, 1))

    def cuts(n, base):
        return pl.ds(base + n * qr, qr)

    def whole(h):
        return cbuf.at[:, p.xat(h)]

    for h in (2, 1, -1, 0):
        s.send((tag, "c", h), part.at[:, p.xat(h), sib], whole(h), p.sibling)
    yield
    for h in (2, 1, -1):
        s.wait((tag, "c", h), whole(h), p.sibling)
        add_into(part.at[:, p.xat(h), core], whole(h))
        s.send((tag, "yb", h), part.at[other, p.xat(h), core, b_], yb.at[h % NX], p.across)
        if h == 2:
            for d, to, n in ways:
                s.send((tag, "xa2", d), part.at[:, p.xat(2), core, cuts(n, 0)], xa2.at[:, cuts(n, 0)], to)
    s.wait((tag, "c", 0), whole(0), p.sibling)
    add_into(part.at[:, p.x, core], whole(0))
    s.send((tag, "yb", 0), part.at[other, p.x, core, b_], yb.at[0], p.across)
    yield
    s.wait((tag, "yb", 2), yb.at[2], p.across)
    add_into(part.at[mine, p.xat(2), core, b_], yb.at[2])
    for d, to, n in ways:
        s.send((tag, "xb2", d), part.at[mine, p.xat(2), core, cuts(n, half)], xb2.at[cuts(n, 0)], to)
    yield
    for d, to, n in ways:
        s.wait((tag, "xa2", d), xa2.at[:, cuts(n, 0)], to)
        add_into(part.at[:, p.xat(d), core, cuts(n, 0)], xa2.at[:, cuts(n, 0)])
        s.send((tag, "xa1", d), part.at[:, p.xat(d), core, a_], xa1.at[n], to)
    yield
    for d, to, n in ways:
        s.wait((tag, "yb", d), yb.at[d % NX], p.across)
        add_into(part.at[mine, p.xat(d), core, b_], yb.at[d % NX])
        s.wait((tag, "xb2", d), xb2.at[cuts(n, 0)], to)
        add_into(part.at[mine, p.xat(d), core, cuts(n, half)], xb2.at[cuts(n, 0)])
        s.send((tag, "xb1", d), part.at[mine, p.xat(d), core, b_], xb1.at[n], to)
    yield
    for d, to, n in ways:
        s.wait((tag, "xa1", d), xa1.at[n], to)
    add_into(part.at[:, p.x, core, a_], xa1.at[0], xa1.at[1])
    s.send((tag, "ya"), part.at[other, p.x, core, a_], ya, p.across)
    s.wait((tag, "yb", 0), yb.at[0], p.across)
    yield
    for d, to, n in ways:
        s.wait((tag, "xb1", d), xb1.at[n], to)
    add_into(part.at[mine, p.x, core, b_], yb.at[0], xb1.at[0], xb1.at[1])
    yield
    s.wait((tag, "ya"), ya, p.across)
    add_into(part.at[mine, p.x, core, a_], ya)


def reduce_col_scratch(n_yh, n_x, rows, feats):
    half = rows // 2
    return [
        pltpu.VMEM((n_yh, n_x, rows, feats), BF16),
        pltpu.VMEM((n_yh, half, feats), BF16),
        pltpu.VMEM((2, n_yh, half, feats), BF16),
        pltpu.VMEM((half, feats), BF16),
        pltpu.VMEM((2, half, feats), BF16),
        pltpu.VMEM((n_x, half, feats), BF16),
        pltpu.VMEM((half, feats), BF16),
    ]


def gather_col(s, p, tag, tab):
    rows = tab.shape[3]
    half = rows // 2
    qr = half // 2
    a_, b_ = pl.ds(0, half), pl.ds(half, half)
    mine, other, core = p.yh, 1 - p.yh, p.core
    ways = ((1, p.right, 0), (-1, p.left, 1))

    def blk(yh, h, ds):
        return tab.at[yh, p.xat(h), core, ds]

    def pair(h, ds):
        return tab.at[:, p.xat(h), core, ds]

    def push(key, b, to):
        s.send((tag,) + key, b, b, to)

    def took(key, b):
        s.wait((tag,) + key, b, p.sibling)

    push(("ya",), blk(mine, 0, a_), p.across)
    for d, to, n in ways:
        push(("b", d), blk(mine, 0, b_), to)
    push(("yb", 0), blk(mine, 0, b_), p.across)
    yield
    took(("ya",), blk(other, 0, a_))
    for d, to, n in ways:
        push(("a", d), pair(0, a_), to)
    push(("c", 0, "a"), pair(0, a_), p.sibling)
    yield
    for d, to, n in ways:
        took(("b", d), blk(mine, -d, b_))
        push(("b2", d), blk(mine, -d, pl.ds(half + n * qr, qr)), to)
        push(("yb", -d), blk(mine, -d, b_), p.across)
    yield
    for d, to, n in ways:
        took(("a", d), pair(-d, a_))
        push(("a2", d), pair(-d, pl.ds(n * qr, qr)), to)
        push(("c", -d, "a"), pair(-d, a_), p.sibling)
    took(("yb", 0), blk(other, 0, b_))
    push(("c", 0, "b"), pair(0, b_), p.sibling)
    yield
    for d, to, n in ways:
        took(("b2", d), blk(mine, 2, pl.ds(half + n * qr, qr)))
    push(("yb", 2), blk(mine, 2, b_), p.across)
    yield
    for d in (1, -1):
        took(("yb", d), blk(other, d, b_))
        push(("c", d, "b"), pair(d, b_), p.sibling)
    yield
    for d, to, n in ways:
        took(("a2", d), pair(2, pl.ds(n * qr, qr)))
    push(("c", 2, "a"), pair(2, a_), p.sibling)
    took(("yb", 2), blk(other, 2, b_))
    push(("c", 2, "b"), pair(2, b_), p.sibling)
    yield
    for h in (0, 1, -1, 2):
        for name, ds in (("a", a_), ("b", b_)):
            s.wait((tag, "c", h, name), tab.at[:, p.xat(h), 1 - core, ds], p.sibling)


def sum_weight(s, p, q, wpart, wc, wd, wy, wz, wtab, scale):
    core, sib = p.core, 1 - p.core
    s.send("wc", wpart.at[:, :, sib], wc, p.sibling)
    yield
    s.wait("wc", wc, p.sibling)
    mine = wpart.at[:, :, core]
    mine[...] = mine[...] + wc[...]
    for dy, h in p.mates:
        yh = p.yh + dy - 2 * p.yh * dy
        s.send(("wd", dy, h), wpart.at[yh, p.xat(h), core], wd.at[dy * NX + h], p.mate(dy, h))
    yield
    total = wpart[p.yh, p.x, core]
    for dy, h in p.mates:
        s.wait(("wd", dy, h), wd.at[dy * NX + h], p.mate(dy, h))
        total = total + wd[dy * NX + h]
    wy[0] = total
    s.send("wy", wy.at[0], wy.at[1], q.across)
    yield
    s.wait("wy", wy.at[1], q.across)
    wz[q.z] = wy[0] + wy[1]
    for h in range(1, NZ):
        s.send(("wz", h), wz.at[q.z], wz.at[q.z], {"row": q.at(q.yl, h)})
    yield
    for h in range(1, NZ):
        s.wait(("wz", h), wz.at[q.zat(-h)], q.across)
    total = wz[0]
    for z in range(1, NZ):
        total = total + wz[z]
    own = wtab.at[p.yh, p.x, core]
    own[...] = total * scale
    for dy, h in p.mates:
        s.send(("w", dy, h), own, own, p.mate(dy, h))
    yield
    for dy, h in p.mates:
        yh = p.yh + dy - 2 * p.yh * dy
        s.wait(("w", dy, h), wtab.at[yh, p.xat(-h), core], p.sibling)
    s.send("ws", wtab.at[:, :, core], wtab.at[:, :, core], p.sibling)
    yield
    s.wait("ws", wtab.at[:, :, sib], p.sibling)


def drain(steps):
    for _ in steps:
        pass


def layer_kernel(
    scale, x_ref, tiles_ref, tr_ref, tc_ref, cnt_ref, w_ref, g_ref, act_ref, grad_ref, wg_ref,
    xtab, etab, tiles, stash, part, back, plan, splan, tr, tc, cnt, w, g, act, wpart, wc, wd, wy, wz, wtab, *rest,
):
    n_col, n_row = 7, 4
    for_col, for_row, (send_sem, recv_sem, sems) = rest[:n_col], rest[n_col : n_col + n_row], rest[n_col + n_row :]
    slots, edge, _ = tiles_ref.shape
    rows, feats = x_ref.shape
    per = rows // edge
    p, q = ColPlace(), RowPlace()
    mr, mc = lax.axis_index("row"), lax.axis_index("col")

    barrier = pltpu.get_barrier_semaphore()
    peers = [p.sibling, q.across] + [p.mate(dy, h) for dy, h in p.mates]
    peers += [{"row": q.at(q.yl, h)} for h in range(1, NZ)]
    for peer in peers:
        pl.semaphore_signal(barrier, inc=1, device_id=peer, device_id_type=MESH)
    loads = [
        pltpu.make_async_copy(tr_ref.at[mr], tr, sems.at[0]),
        pltpu.make_async_copy(tc_ref.at[mr], tc, sems.at[1]),
        pltpu.make_async_copy(cnt_ref, cnt, sems.at[2]),
        pltpu.make_async_copy(x_ref, xtab.at[q.yl, q.z], sems.at[3]),
        pltpu.make_async_copy(tiles_ref, tiles.at[pl.ds(0, slots)], sems.at[4]),
        pltpu.make_async_copy(w_ref, w, sems.at[5]),
        pltpu.make_async_copy(g_ref, g, sems.at[6]),
    ]
    for c in loads:
        c.start()
    tiles[slots] = jnp.zeros((edge, edge), tiles.dtype)
    loads[3].wait()
    pl.semaphore_wait(barrier, len(peers))

    s = Sender(send_sem, recv_sem)
    gather = gather_row(s, q, "gr", xtab)
    next(gather)
    for c in loads[:3]:
        c.wait()
    n_tiles = stash.shape[0] * 2 - 2 - slots
    order_slots(tr[pl.ds(mc, 1)], tc[pl.ds(mc, 1)], cnt[mr, mc], n_tiles, plan)
    to_scalars = pltpu.make_async_copy(plan, splan, sems.at[7])
    to_scalars.start()
    drain(gather)
    to_scalars.wait()
    for c in loads[4:]:
        c.wait()

    multiply(False, splan, tiles, xtab.reshape(n_tiles, edge, feats), stash)
    for t in range(n_tiles):
        b = t // per
        part[b // (2 * NX), b // 2 % NX, b % 2, pl.ds(t % per * edge, edge)] = stash[splan[3, t]]
    drain(reduce_col(s, p, "rc", part, *for_col))

    agg = part[p.yh, p.x, p.core]
    pre = jnp.dot(agg, w[...], preferred_element_type=F32)
    logistic = jax.nn.sigmoid(pre)
    upstream = g[...].astype(F32)
    d_pre = (upstream * logistic * (1.0 + pre * (1.0 - logistic))).astype(BF16)
    e = lax.dot_general(d_pre, w[...], (((1,), (1,)), ((), ())), preferred_element_type=F32)
    etab[p.yh, p.x, p.core] = e.astype(BF16)
    gather = gather_col(s, p, "gc", etab)
    next(gather)
    act[...] = (pre * logistic).astype(BF16)
    act_out = pltpu.make_async_copy(act, act_ref, sems.at[8])
    act_out.start()
    wg = lax.dot_general(agg, d_pre, (((0,), (0,)), ((), ())), preferred_element_type=F32)
    wpart[...] = wg.reshape(wpart.shape)
    weights = sum_weight(s, p, q, wpart, wc, wd, wy, wz, wtab, scale)
    next(weights)
    next(gather)
    next(gather)
    next(weights)
    drain(gather)
    next(weights)

    multiply(True, splan, tiles, etab.reshape(n_tiles, edge, feats), stash)
    next(weights)
    for t in range(n_tiles):
        b = t // per
        back[b // NZ, b % NZ, pl.ds(t % per * edge, edge)] = stash[splan[7, t]]
    reduce = reduce_row(s, q, "rr", back, *for_row)
    for _ in range(4):
        next(reduce)
    next(weights)
    for _ in range(3):
        next(reduce)
    next(weights)
    drain(reduce)
    grad_out = pltpu.make_async_copy(back.at[q.yl, q.z], grad_ref, sems.at[9])
    grad_out.start()
    drain(weights)
    wg_out = pltpu.make_async_copy(wtab, wg_ref, sems.at[10])
    wg_out.start()
    s.finish()
    for c in (act_out, grad_out, wg_out):
        c.wait()


def layer(x, tiles, tile_rows, tile_cols, tile_count, weight, cot):
    rows, feats = x.shape
    slots, edge, _ = tiles.shape
    n_row, n_col, _ = tile_rows.shape
    n_yh = n_col // (2 * NX)
    n_tiles = n_col * rows // edge
    steps = (slots + n_tiles) // 2
    n_w = feats // n_col
    hbm = pl.BlockSpec(memory_space=pl.ANY)
    vmem = pltpu.VMEM
    return pl.pallas_call(
        functools.partial(layer_kernel, 1.0 / math.sqrt(rows * n_row * n_col)),
        out_shape=(
            jax.ShapeDtypeStruct((rows, feats), BF16),
            jax.ShapeDtypeStruct((rows, feats), BF16),
            jax.ShapeDtypeStruct((n_yh, NX, 2, n_w, feats), F32),
        ),
        in_specs=[hbm] * 7,
        out_specs=(hbm, hbm, hbm),
        scratch_shapes=[
            vmem((n_row // NZ, NZ, rows, feats), BF16),
            vmem((n_yh, NX, 2, rows, feats), BF16),
            vmem((slots + 1, edge, edge), BF16),
            vmem((steps + 1, edge, feats), BF16),
            vmem((n_yh, NX, 2, rows, feats), BF16),
            vmem((n_row // NZ, NZ, rows, feats), BF16),
            vmem((8, PLACES), jnp.int32),
            pltpu.SMEM((8, PLACES), jnp.int32),
            vmem((n_col, slots), jnp.int32),
            vmem((n_col, slots), jnp.int32),
            pltpu.SMEM((n_row, n_col), jnp.int32),
            vmem((feats, feats), BF16),
            vmem((rows, feats), BF16),
            vmem((rows, feats), BF16),
            vmem((n_yh, NX, 2, n_w, feats), F32),
            vmem((n_yh, NX, n_w, feats), F32),
            vmem((n_yh * NX, n_w, feats), F32),
            vmem((2, n_w, feats), F32),
            vmem((NZ, n_w, feats), F32),
            vmem((n_yh, NX, 2, n_w, feats), F32),
        ]
        + reduce_col_scratch(n_yh, NX, rows, feats)
        + reduce_row_scratch(rows, feats)
        + [
            pltpu.SemaphoreType.DMA((200,)),
            pltpu.SemaphoreType.DMA((200,)),
            pltpu.SemaphoreType.DMA((11,)),
        ],
        compiler_params=pltpu.CompilerParams(
            collective_id=1, has_side_effects=True, vmem_limit_bytes=56 << 20
        ),
        name="layer",
    )(x, tiles, tile_rows, tile_cols, tile_count, weight, cot)


def per_device(node_features, tile_values, tile_rows, tile_cols, tile_count, weight, cotangent):
    act, grad, wgrad = layer(
        node_features[0, 0], tile_values[0, 0], tile_rows, tile_cols, tile_count, weight, cotangent[0, 0]
    )
    return act[None, None], grad[None, None], wgrad.reshape(weight.shape)


def solution(mesh):
    in_specs = (
        P("col", "row", None, None),
        P("row", "col", None, None, None),
        P(),
        P(),
        P(),
        P(),
        P("row", "col", None, None),
    )
    out_specs = (P("row", "col", None, None), P("col", "row", None, None), P())
    return jax.shard_map(
        per_device, mesh=mesh, in_specs=in_specs, out_specs=out_specs, check_vma=False
    )
```

time: 668 us -> 104 us (0.16); the launches traced: 656 us -> 104 us
  waiting for transfers between devices: 515 us -> 0 us
  Pallas kernels: 0 us -> 98.3 us
  other arithmetic: 69 us -> 0 us
  matrix products: 27.3 us -> 0 us
  local copies, waits for them, and re-layouts: 29.3 us -> 4.8 us
  between operations: 14.4 us -> 0.64 us
    reduce_scatter x2 -> x0, waiting for transfers between devices: 207 us -> none  [the longest x1 143 us: per_device(): lax.psum_scatter(partial_value, 'col', scatter_dimension=0, tiled=True)]
    psum x1 -> x0, waiting for transfers between devices: 197 us -> none  [per_device(): lax.psum(weight_part, ('row', 'col'))]
    all_gather x2 -> x0, waiting for transfers between devices: 110 us -> none  [the longest x1 64.9 us: per_device(): gathered = lax.all_gather(node_features, 'row', axis=1, tiled=True)]
    pallas_call x0 -> x1, Pallas kernels: none -> 98.3 us  [layer(): pl.pallas_call(functools.partial(layer_kernel, 1.0 / math.sqrt(rows * n_r...]
    scatter-add x6 -> x0, other arithmetic: 59.5 us -> none  [advance(): return running.at[places].add(product, mode='drop')]
    dot_general x9 -> x0, matrix products: 27.3 us -> none  [the longest x6 23.6 us: advance(): jnp.einsum(pattern, tile_block, operand, preferred_element_type=jnp.float32)]
    gather x6 -> x0, local copies, waits for them, and re-layouts: 13.7 us -> none  [advance(): operand = table[picked]]
  transfers between devices with their start and end apart: 5 -> 0, of which waited for: 5 -> 0; matrix products, arithmetic and copies ran while one was open for 11% -> 0% of each run, Pallas kernels for 0% -> 0%
where the time goes in v3:
time: 104 us
  Pallas kernels  98.3 us (95%)
  local copies, waits for them, and re-layouts  4.8 us (5%)
    pallas_call x1, Pallas kernels, layer(): pl.pallas_call(functools.partial(layer_kernel, 1.0 / math.sqrt(rows * n_r...  98.3 us
    unnamed x3, local copies, waits for them, and re-layouts  4.8 us

profile of v3, /device:TPU:1, one launch (start us, length us, event | category | flops | bytes accessed | tf_op | source)
XLA Modules:
  0.0 103.8 jit_solution(13307429422203956153)
XLA Ops:
  0.6 98.3 %layer.1 = (bf16[256,256]{1,0:T(8,128)(2,1)}, bf16[256,256]{1,0:T(8,128)(2,1)}, f32[2,4,2,16,256]{4,3,2,1,0:T(8,128)}) custom-call(bf16[256,256]{1,0:T(8,128)(2,1)} %bitcast.8, bf16[192,128,128]{2,1,0:T(8,128)(2,1)} %bitcast.6, s32[16,16,192]{2,1,0:T(8,128)} %tr_ref.1, s32[16,16,192]{2,1,0:T(8,128)} %tc_ref.1, s32[16,16]{1,0:T(8,128)} %cnt_ref.1, ...), custom_call_target="tpu_custom_call" | custom-call | tf_op jit(solution)/shard_map/layer/pallas_call | solution.py:573
  99.0 1.6 %copy.13 = bf16[1,1,256,256]{3,2,1,0:T(8,128)(2,1)} copy(bf16[1,1,256,256]{3,2,1,0:T(8,128)(2,1)} %bitcast.11) | data formatting | bytes 262144
  100.6 1.6 %copy.14 = bf16[1,1,256,256]{3,2,1,0:T(8,128)(2,1)} copy(bf16[1,1,256,256]{3,2,1,0:T(8,128)(2,1)} %bitcast.10) | data formatting | bytes 262144
  102.1 1.7 %copy.15 = f32[256,256]{1,0:T(8,128)} copy(f32[256,256]{1,0:T(8,128)} %bitcast.7) | data formatting | bytes 524288

commit v4 on v3

--- a/solution.py
+++ b/solution.py
@@ -129,7 +129,7 @@
         plan[pl.ds(n, 1)] = x
 
 
-GROUP = 16
+GROUP = 28
 
 
 def multiply(flip, plan, tiles, tab, stash):
@@ -162,138 +162,139 @@
     dst[...] = total.astype(dst.dtype)
 
 
-def cut_of(rows):
-    return (rows * 7 // 16) // 16 * 16
+def row_parts(rows):
+    cut = (rows * 7 // 16) // 16 * 16
+    rest = rows - cut
+    return (0, cut, cut // 2 // 16 * 16), (cut, rest, -(-rest // 2 // 16) * 16)
+
+
+def hop_rows(part, d, h):
+    base, n, half = part
+    if h < NZ // 2:
+        return base, n
+    return (base, half) if d == 1 else (base + half, n - half)
 
 
 def gather_row(s, p, tag, tab):
-    rows = tab.shape[2]
-    cut = cut_of(rows)
+    first, rest = row_parts(tab.shape[2])
     top = NZ // 2
     mine, other = p.yl, 1 - p.yl
     ways = ((1, p.right), (-1, p.left))
-    a_, b_ = pl.ds(0, cut), pl.ds(cut, rows - cut)
-    a_last = {1: pl.ds(0, cut // 2 // 16 * 16 + 16), -1: pl.ds(cut // 2 // 16 * 16 + 16, cut - cut // 2 // 16 * 16 - 16)}
-    b_half = (rows - cut) // 2 // 16 * 16
-    b_last = {1: pl.ds(cut, b_half), -1: pl.ds(cut + b_half, rows - cut - b_half)}
 
     def blk(yl, h, ds):
-        return tab.at[yl, p.zat(h), ds]
-
-    def pair(h, ds):
-        return tab.at[:, p.zat(h), ds]
+        return tab.at[yl, p.zat(h), pl.ds(*ds)]
 
     def push(key, b, to):
         s.send((tag,) + key, b, b, to)
 
-    push(("ya",), blk(mine, 0, a_), p.across)
-    for d, to in ways:
-        push(("b", d, 1), blk(mine, 0, b_), to)
-    push(("yb", 0), blk(mine, 0, b_), p.across)
-    yield
-    s.wait((tag, "ya"), blk(other, 0, a_), p.across)
-    for d, to in ways:
-        push(("a", d, 1), pair(0, a_), to)
+    streams = (("b", mine, rest), ("a", mine, first), ("c", other, first))
+
+    def hop(name, yl, part, h):
+        for d, to in ways:
+            push((name, d, h), blk(yl, d * (1 - h), hop_rows(part, d, h)), to)
+
+    push(("ya",), blk(mine, 0, first[:2]), p.across)
+    for name, yl, part in streams[:2]:
+        hop(name, yl, part, 1)
+    push(("yb", 0), blk(mine, 0, rest[:2]), p.across)
+    yield
+    s.wait((tag, "ya"), blk(other, 0, first[:2]), p.across)
+    hop(*streams[2], 1)
     for h in range(1, top + 1):
-        yield
-        for d, to in ways:
-            s.wait((tag, "b", d, h), blk(mine, -d * h, b_last[d] if h == top else b_), to)
-            if h < top:
-                push(("b", d, h + 1), blk(mine, -d * h, b_last[d] if h == top - 1 else b_), to)
-                push(("yb", -d * h), blk(mine, -d * h, b_), p.across)
-        if h == top:
-            push(("yb", top), blk(mine, top, b_), p.across)
-        yield
-        for d, to in ways:
-            s.wait((tag, "a", d, h), pair(-d * h, a_last[d] if h == top else a_), to)
-            if h < top:
-                push(("a", d, h + 1), pair(-d * h, a_last[d] if h == top - 1 else a_), to)
+        for name, yl, part in streams:
+            yield
+            for d, to in ways:
+                s.wait((tag, name, d, h), blk(yl, -d * h, hop_rows(part, d, h)), to)
+                if h < top:
+                    push((name, d, h + 1), blk(yl, -d * h, hop_rows(part, d, h + 1)), to)
+                if name == "b" and (h < top or d == -1):
+                    push(("yb", -d * h), blk(mine, -d * h, rest[:2]), p.across)
     yield
     for h in [0] + [d * h for h in range(1, top) for d in (1, -1)] + [top]:
-        s.wait((tag, "yb", h), blk(other, h, b_), p.across)
-
-
-def reduce_row(s, p, tag, part, ybuf, abuf, bbuf, fbuf):
-    rows = part.shape[2]
-    cut = cut_of(rows)
+        s.wait((tag, "yb", h), blk(other, h, rest[:2]), p.across)
+
+
+def reduce_row(s, p, tag, part, ybuf, abuf, cbuf, bbuf, fbuf):
+    first, rest = row_parts(part.shape[2])
     top = NZ // 2
     mine, other = p.yl, 1 - p.yl
     ways = ((1, p.right, 0), (-1, p.left, 1))
-    a_, b_ = pl.ds(0, cut), pl.ds(cut, rows - cut)
-    a_mid = cut // 2 // 16 * 16 + 16
-    b_mid = (rows - cut) // 2 // 16 * 16
-    a_last = {1: (0, a_mid), -1: (a_mid, cut)}
-    b_last = {1: (0, b_mid), -1: (b_mid, rows - cut)}
-
-    def a_cut(d, h):
-        lo, hi = a_last[d] if h == top else (0, cut)
-        return pl.ds(lo, hi - lo)
-
-    def b_cut(d, h, base=0):
-        lo, hi = b_last[d] if h == top else (0, rows - cut)
-        return pl.ds(base + lo, hi - lo)
-
-    for h in [top] + [d * h for h in range(top - 1, 0, -1) for d in (1, -1)] + [0]:
-        s.send((tag, "yb", h), part.at[other, p.zat(h), b_], ybuf.at[h + top - 1], p.across)
-        if h == top:
+    streams = (("c", other, first, cbuf), ("a", mine, first, abuf), ("b", mine, rest, bbuf))
+
+    def blk(yl, h, ds):
+        return part.at[yl, p.zat(h), pl.ds(*ds)]
+
+    def hop(name, yl, piece, buf, d, to, n, h):
+        lo, m = hop_rows(piece, d, h)
+        s.send((tag, name, d, h), blk(yl, d * h, (lo, m)), buf.at[h - 1, n, pl.ds(lo - piece[0], m)], to)
+
+    def crossed(h):
+        s.wait((tag, "yb", h), ybuf.at[h + top - 1], p.across)
+        add_into(blk(mine, h, rest[:2]), ybuf.at[h + top - 1])
+
+    s.send((tag, "yb", top), blk(other, top, rest[:2]), ybuf.at[2 * top - 1], p.across)
+    for st in streams[:2]:
+        for w in ways:
+            hop(*st, *w, top)
+    for h in [d * h for h in range(top - 1, 0, -1) for d in (1, -1)] + [0]:
+        s.send((tag, "yb", h), blk(other, h, rest[:2]), ybuf.at[h + top - 1], p.across)
+    yield
+    crossed(top)
+    for w in ways:
+        hop(*streams[2], *w, top)
+    for h in range(top - 1, 0, -1):
+        for name, yl, piece, buf in streams:
+            yield
             for d, to, n in ways:
-                ds = a_cut(d, top)
-                s.send((tag, "a", d, top), part.at[:, p.zat(top), ds], abuf.at[top - 1, n, :, ds], to)
-    for h in range(top, 0, -1):
+                if name == "b":
+                    crossed(d * h)
+                lo, m = hop_rows(piece, d, h + 1)
+                got = buf.at[h, n, pl.ds(lo - piece[0], m)]
+                s.wait((tag, name, d, h + 1), got, to)
+                add_into(blk(yl, d * h, (lo, m)), got)
+                hop(name, yl, piece, buf, d, to, n, h)
+    for name, yl, piece, buf in streams:
         yield
         for d, to, n in ways:
-            if h < top:
-                ds = a_cut(d, h + 1)
-                got = abuf.at[h, n, :, ds]
-                s.wait((tag, "a", d, h + 1), got, to)
-                add_into(part.at[:, p.zat(d * h), ds], got)
-                s.send((tag, "a", d, h), part.at[:, p.zat(d * h), a_], abuf.at[h - 1, n], to)
-        yield
-        for d, to, n in ways:
-            if h < top or d == 1:
-                s.wait((tag, "yb", d * h), ybuf.at[d * h + top - 1], p.across)
-                add_into(part.at[mine, p.zat(d * h), b_], ybuf.at[d * h + top - 1])
-            if h < top:
-                got = bbuf.at[h, n, b_cut(d, h + 1)]
-                s.wait((tag, "b", d, h + 1), got, to)
-                add_into(part.at[mine, p.zat(d * h), b_cut(d, h + 1, cut)], got)
-            ds = b_cut(d, h)
-            s.send((tag, "b", d, h), part.at[mine, p.zat(d * h), b_cut(d, h, cut)], bbuf.at[h - 1, n, ds], to)
-    yield
-    for d, to, n in ways:
-        s.wait((tag, "a", d, 1), abuf.at[0, n], to)
-    add_into(part.at[:, p.z, a_], abuf.at[0, 0], abuf.at[0, 1])
-    s.send((tag, "f"), part.at[other, p.z, a_], fbuf, p.across)
-    s.wait((tag, "yb", 0), ybuf.at[top - 1], p.across)
-    yield
-    for d, to, n in ways:
-        s.wait((tag, "b", d, 1), bbuf.at[0, n], to)
-    add_into(part.at[mine, p.z, b_], ybuf.at[top - 1], bbuf.at[0, 0], bbuf.at[0, 1])
+            s.wait((tag, name, d, 1), buf.at[0, n], to)
+        if name == "b":
+            crossed(0)
+        add_into(blk(yl, 0, piece[:2]), buf.at[0, 0], buf.at[0, 1])
+        if name == "c":
+            s.send((tag, "f"), blk(other, 0, first[:2]), fbuf, p.across)
     yield
     s.wait((tag, "f"), fbuf, p.across)
-    add_into(part.at[mine, p.z, a_], fbuf)
+    add_into(blk(mine, 0, first[:2]), fbuf)
 
 
 def reduce_row_scratch(rows, feats):
-    cut, top = cut_of(rows), NZ // 2
+    (_, m, _), (_, n, _) = row_parts(rows)
+    top = NZ // 2
     return [
-        pltpu.VMEM((NZ, rows - cut, feats), BF16),
-        pltpu.VMEM((top, 2, 2, cut, feats), BF16),
-        pltpu.VMEM((top, 2, rows - cut, feats), BF16),
-        pltpu.VMEM((cut, feats), BF16),
+        pltpu.VMEM((NZ, n, feats), BF16),
+        pltpu.VMEM((top, 2, m, feats), BF16),
+        pltpu.VMEM((top, 2, m, feats), BF16),
+        pltpu.VMEM((top, 2, n, feats), BF16),
+        pltpu.VMEM((m, feats), BF16),
     ]
 
 
+def col_parts(rows):
+    na = rows * 3 // 8 // 32 * 32
+    return na, rows - na
+
+
 def reduce_col(s, p, tag, part, cbuf, xa2, xa1, xb2, xb1, yb, ya):
-    rows = part.shape[3]
-    half = rows // 2
-    qr = half // 2
-    a_, b_ = pl.ds(0, half), pl.ds(half, half)
+    na, nb = col_parts(part.shape[3])
+    a_, b_ = pl.ds(0, na), pl.ds(na, nb)
     mine, other, core, sib = p.yh, 1 - p.yh, p.core, 1 - p.core
     ways = ((1, p.right, 0), (-1, p.left, 1))
 
-    def cuts(n, base):
-        return pl.ds(base + n * qr, qr)
+    def a_cut(n):
+        return pl.ds(n * (na // 2), na // 2)
+
+    def b_cut(n, base):
+        return pl.ds(base + n * (nb // 2), nb // 2)
 
     def whole(h):
         return cbuf.at[:, p.xat(h)]
@@ -307,26 +308,26 @@
         s.send((tag, "yb", h), part.at[other, p.xat(h), core, b_], yb.at[h % NX], p.across)
         if h == 2:
             for d, to, n in ways:
-                s.send((tag, "xa2", d), part.at[:, p.xat(2), core, cuts(n, 0)], xa2.at[:, cuts(n, 0)], to)
+                s.send((tag, "xa2", d), part.at[:, p.xat(2), core, a_cut(n)], xa2.at[:, a_cut(n)], to)
     s.wait((tag, "c", 0), whole(0), p.sibling)
     add_into(part.at[:, p.x, core], whole(0))
     s.send((tag, "yb", 0), part.at[other, p.x, core, b_], yb.at[0], p.across)
     yield
+    for d, to, n in ways:
+        s.wait((tag, "xa2", d), xa2.at[:, a_cut(n)], to)
+        add_into(part.at[:, p.xat(d), core, a_cut(n)], xa2.at[:, a_cut(n)])
+        s.send((tag, "xa1", d), part.at[:, p.xat(d), core, a_], xa1.at[n], to)
+    yield
     s.wait((tag, "yb", 2), yb.at[2], p.across)
     add_into(part.at[mine, p.xat(2), core, b_], yb.at[2])
     for d, to, n in ways:
-        s.send((tag, "xb2", d), part.at[mine, p.xat(2), core, cuts(n, half)], xb2.at[cuts(n, 0)], to)
-    yield
-    for d, to, n in ways:
-        s.wait((tag, "xa2", d), xa2.at[:, cuts(n, 0)], to)
-        add_into(part.at[:, p.xat(d), core, cuts(n, 0)], xa2.at[:, cuts(n, 0)])
-        s.send((tag, "xa1", d), part.at[:, p.xat(d), core, a_], xa1.at[n], to)
+        s.send((tag, "xb2", d), part.at[mine, p.xat(2), core, b_cut(n, na)], xb2.at[b_cut(n, 0)], to)
     yield
     for d, to, n in ways:
         s.wait((tag, "yb", d), yb.at[d % NX], p.across)
         add_into(part.at[mine, p.xat(d), core, b_], yb.at[d % NX])
-        s.wait((tag, "xb2", d), xb2.at[cuts(n, 0)], to)
-        add_into(part.at[mine, p.xat(d), core, cuts(n, half)], xb2.at[cuts(n, 0)])
+        s.wait((tag, "xb2", d), xb2.at[b_cut(n, 0)], to)
+        add_into(part.at[mine, p.xat(d), core, b_cut(n, na)], xb2.at[b_cut(n, 0)])
         s.send((tag, "xb1", d), part.at[mine, p.xat(d), core, b_], xb1.at[n], to)
     yield
     for d, to, n in ways:
@@ -344,23 +345,21 @@
 
 
 def reduce_col_scratch(n_yh, n_x, rows, feats):
-    half = rows // 2
+    na, nb = col_parts(rows)
     return [
         pltpu.VMEM((n_yh, n_x, rows, feats), BF16),
-        pltpu.VMEM((n_yh, half, feats), BF16),
-        pltpu.VMEM((2, n_yh, half, feats), BF16),
-        pltpu.VMEM((half, feats), BF16),
-        pltpu.VMEM((2, half, feats), BF16),
-        pltpu.VMEM((n_x, half, feats), BF16),
-        pltpu.VMEM((half, feats), BF16),
+        pltpu.VMEM((n_yh, na, feats), BF16),
+        pltpu.VMEM((2, n_yh, na, feats), BF16),
+        pltpu.VMEM((nb, feats), BF16),
+        pltpu.VMEM((2, nb, feats), BF16),
+        pltpu.VMEM((n_x, nb, feats), BF16),
+        pltpu.VMEM((na, feats), BF16),
     ]
 
 
 def gather_col(s, p, tag, tab):
-    rows = tab.shape[3]
-    half = rows // 2
-    qr = half // 2
-    a_, b_ = pl.ds(0, half), pl.ds(half, half)
+    na, nb = col_parts(tab.shape[3])
+    a_, b_ = pl.ds(0, na), pl.ds(na, nb)
     mine, other, core = p.yh, 1 - p.yh, p.core
     ways = ((1, p.right, 0), (-1, p.left, 1))
 
@@ -388,18 +387,18 @@
     yield
     for d, to, n in ways:
         took(("b", d), blk(mine, -d, b_))
-        push(("b2", d), blk(mine, -d, pl.ds(half + n * qr, qr)), to)
+        push(("b2", d), blk(mine, -d, pl.ds(na + n * (nb // 2), nb // 2)), to)
         push(("yb", -d), blk(mine, -d, b_), p.across)
     yield
     for d, to, n in ways:
         took(("a", d), pair(-d, a_))
-        push(("a2", d), pair(-d, pl.ds(n * qr, qr)), to)
+        push(("a2", d), pair(-d, pl.ds(n * (na // 2), na // 2)), to)
         push(("c", -d, "a"), pair(-d, a_), p.sibling)
     took(("yb", 0), blk(other, 0, b_))
     push(("c", 0, "b"), pair(0, b_), p.sibling)
     yield
     for d, to, n in ways:
-        took(("b2", d), blk(mine, 2, pl.ds(half + n * qr, qr)))
+        took(("b2", d), blk(mine, 2, pl.ds(na + n * (nb // 2), nb // 2)))
     push(("yb", 2), blk(mine, 2, b_), p.across)
     yield
     for d in (1, -1):
@@ -407,7 +406,7 @@
         push(("c", d, "b"), pair(d, b_), p.sibling)
     yield
     for d, to, n in ways:
-        took(("a2", d), pair(2, pl.ds(n * qr, qr)))
+        took(("a2", d), pair(2, pl.ds(n * (na // 2), na // 2)))
     push(("c", 2, "a"), pair(2, a_), p.sibling)
     took(("yb", 2), blk(other, 2, b_))
     push(("c", 2, "b"), pair(2, b_), p.sibling)
@@ -463,11 +462,19 @@
         pass
 
 
+def drain_after(s, steps):
+    before, s.sent = s.sent, []
+    next(steps)
+    for c in before:
+        c.wait_send()
+    drain(steps)
+
+
 def layer_kernel(
     scale, x_ref, tiles_ref, tr_ref, tc_ref, cnt_ref, w_ref, g_ref, act_ref, grad_ref, wg_ref,
-    xtab, etab, tiles, stash, part, back, plan, splan, tr, tc, cnt, w, g, act, wpart, wc, wd, wy, wz, wtab, *rest,
+    xtab, etab, tiles, stash, part, back, plan, splan, tr, tc, cnt, w, g, wpart, wc, wd, wy, wz, *rest,
 ):
-    n_col, n_row = 7, 4
+    n_col, n_row = 7, 5
     for_col, for_row, (send_sem, recv_sem, sems) = rest[:n_col], rest[n_col : n_col + n_row], rest[n_col + n_row :]
     slots, edge, _ = tiles_ref.shape
     rows, feats = x_ref.shape
@@ -492,18 +499,17 @@
     for c in loads:
         c.start()
     tiles[slots] = jnp.zeros((edge, edge), tiles.dtype)
-    loads[3].wait()
-    pl.semaphore_wait(barrier, len(peers))
-
-    s = Sender(send_sem, recv_sem)
-    gather = gather_row(s, q, "gr", xtab)
-    next(gather)
+    n_tiles = stash.shape[0] * 2 - 2 - slots
     for c in loads[:3]:
         c.wait()
-    n_tiles = stash.shape[0] * 2 - 2 - slots
     order_slots(tr[pl.ds(mc, 1)], tc[pl.ds(mc, 1)], cnt[mr, mc], n_tiles, plan)
     to_scalars = pltpu.make_async_copy(plan, splan, sems.at[7])
     to_scalars.start()
+    loads[3].wait()
+    pl.semaphore_wait(barrier, len(peers))
+
+    s = Sender(send_sem, recv_sem)
+    gather = gather_row(s, q, "gr", xtab)
     drain(gather)
     to_scalars.wait()
     for c in loads[4:]:
@@ -513,7 +519,8 @@
     for t in range(n_tiles):
         b = t // per
         part[b // (2 * NX), b // 2 % NX, b % 2, pl.ds(t % per * edge, edge)] = stash[splan[3, t]]
-    drain(reduce_col(s, p, "rc", part, *for_col))
+    reduce = reduce_col(s, p, "rc", part, *for_col)
+    drain_after(s, reduce)
 
     agg = part[p.yh, p.x, p.core]
     pre = jnp.dot(agg, w[...], preferred_element_type=F32)
@@ -522,15 +529,16 @@
     d_pre = (upstream * logistic * (1.0 + pre * (1.0 - logistic))).astype(BF16)
     e = lax.dot_general(d_pre, w[...], (((1,), (1,)), ((), ())), preferred_element_type=F32)
     etab[p.yh, p.x, p.core] = e.astype(BF16)
+    before, s.sent = s.sent, []
     gather = gather_col(s, p, "gc", etab)
     next(gather)
-    act[...] = (pre * logistic).astype(BF16)
-    act_out = pltpu.make_async_copy(act, act_ref, sems.at[8])
-    act_out.start()
+    act_ref[...] = (pre * logistic).astype(BF16)
     wg = lax.dot_general(agg, d_pre, (((0,), (0,)), ((), ())), preferred_element_type=F32)
     wpart[...] = wg.reshape(wpart.shape)
-    weights = sum_weight(s, p, q, wpart, wc, wd, wy, wz, wtab, scale)
+    weights = sum_weight(s, p, q, wpart, wc, wd, wy, wz, wg_ref, scale)
     next(weights)
+    for c in before:
+        c.wait_send()
     next(gather)
     next(gather)
     next(weights)
@@ -542,25 +550,25 @@
     for t in range(n_tiles):
         b = t // per
         back[b // NZ, b % NZ, pl.ds(t % per * edge, edge)] = stash[splan[7, t]]
+    before, s.sent = s.sent, []
     reduce = reduce_row(s, q, "rr", back, *for_row)
-    for _ in range(4):
-        next(reduce)
-    next(weights)
+    next(reduce)
+    for c in before:
+        c.wait_send()
     for _ in range(3):
         next(reduce)
     next(weights)
+    for _ in range(5):
+        next(reduce)
+    next(weights)
     drain(reduce)
-    grad_out = pltpu.make_async_copy(back.at[q.yl, q.z], grad_ref, sems.at[9])
-    grad_out.start()
+    grad_ref[...] = back[q.yl, q.z]
     drain(weights)
-    wg_out = pltpu.make_async_copy(wtab, wg_ref, sems.at[10])
-    wg_out.start()
     s.finish()
-    for c in (act_out, grad_out, wg_out):
-        c.wait()
-
-
-def layer(x, tiles, tile_rows, tile_cols, tile_count, weight, cot):
+
+
+def layer(*args):
+    x, tiles, tile_rows = args[:3]
     rows, feats = x.shape
     slots, edge, _ = tiles.shape
     n_row, n_col, _ = tile_rows.shape
@@ -568,17 +576,17 @@
     n_tiles = n_col * rows // edge
     steps = (slots + n_tiles) // 2
     n_w = feats // n_col
-    hbm = pl.BlockSpec(memory_space=pl.ANY)
+    hbm = pl.BlockSpec(memory_space=pltpu.HBM)
     vmem = pltpu.VMEM
     return pl.pallas_call(
         functools.partial(layer_kernel, 1.0 / math.sqrt(rows * n_row * n_col)),
         out_shape=(
-            jax.ShapeDtypeStruct((rows, feats), BF16),
-            jax.ShapeDtypeStruct((rows, feats), BF16),
-            jax.ShapeDtypeStruct((n_yh, NX, 2, n_w, feats), F32),
+            vmem((rows, feats), BF16),
+            vmem((rows, feats), BF16),
+            vmem((n_yh, NX, 2, n_w, feats), F32),
         ),
         in_specs=[hbm] * 7,
-        out_specs=(hbm, hbm, hbm),
+        out_specs=[pl.BlockSpec(memory_space=vmem)] * 3,
         scratch_shapes=[
             vmem((n_row // NZ, NZ, rows, feats), BF16),
             vmem((n_yh, NX, 2, rows, feats), BF16),
@@ -593,26 +601,24 @@
             pltpu.SMEM((n_row, n_col), jnp.int32),
             vmem((feats, feats), BF16),
             vmem((rows, feats), BF16),
-            vmem((rows, feats), BF16),
             vmem((n_yh, NX, 2, n_w, feats), F32),
             vmem((n_yh, NX, n_w, feats), F32),
             vmem((n_yh * NX, n_w, feats), F32),
             vmem((2, n_w, feats), F32),
             vmem((NZ, n_w, feats), F32),
-            vmem((n_yh, NX, 2, n_w, feats), F32),
         ]
         + reduce_col_scratch(n_yh, NX, rows, feats)
         + reduce_row_scratch(rows, feats)
         + [
             pltpu.SemaphoreType.DMA((200,)),
             pltpu.SemaphoreType.DMA((200,)),
-            pltpu.SemaphoreType.DMA((11,)),
+            pltpu.SemaphoreType.DMA((8,)),
         ],
         compiler_params=pltpu.CompilerParams(
-            collective_id=1, has_side_effects=True, vmem_limit_bytes=56 << 20
+            collective_id=1, has_side_effects=True, vmem_limit_bytes=48 << 20
         ),
         name="layer",
-    )(x, tiles, tile_rows, tile_cols, tile_count, weight, cot)
+    )(*[pltpu.with_memory_space_constraint(a, pltpu.HBM) for a in args])
 
 
 def per_device(node_features, tile_values, tile_rows, tile_cols, tile_count, weight, cotangent):

time: 104 us -> 94.2 us (0.906)
  Pallas kernels: 98.3 us -> 91.3 us
  local copies, waits for them, and re-layouts: 4.8 us -> 2.01 us
    pallas_call x1, Pallas kernels: 98.3 us -> 91.3 us  [layer(): pl.pallas_call(functools.partial(layer_kernel, 1.0 / math.sqrt(rows * n_r...]
    unnamed x3, local copies, waits for them, and re-layouts: 4.8 us -> 2.01 us
where the time goes in v4:
time: 94.2 us; the launch traced here: 94 us
  Pallas kernels  91.3 us (97%)
  local copies, waits for them, and re-layouts  2.01 us (2%)
    pallas_call x1, Pallas kernels, layer(): pl.pallas_call(functools.partial(layer_kernel, 1.0 / math.sqrt(rows * n_r...  91.3 us
    unnamed x3, local copies, waits for them, and re-layouts  2.01 us

profile of v4, /device:TPU:1, one launch (start us, length us, event | category | flops | bytes accessed | tf_op | source)
XLA Modules:
  0.0 94.0 jit_solution(9564214129686527594)
XLA Ops:
  0.6 91.3 %layer.1 = (bf16[256,256]{1,0:T(8,128)(2,1)S(1)}, bf16[256,256]{1,0:T(8,128)(2,1)S(1)}, f32[2,4,2,16,256]{4,3,2,1,0:T(8,128)S(1)}) custom-call(bf16[256,256]{1,0:T(8,128)(2,1)} %bitcast.10, bf16[192,128,128]{2,1,0:T(8,128)(2,1)} %bitcast.9, s32[16,16,192]{2,1,0:T(8,128)} %tr_ref.1, s32[16,16,192]{2,1,0:T(8,128)} %tc_ref.1, s32[16,16]{1,0:T(8,128)} %cnt_ref.1, ...), custom_call_target="tpu_custom_call" | custom-call | tf_op jit(solution)/shard_map/layer/pallas_call | solution.py:581
  92.0 0.7 copy.13
  92.6 0.7 copy.14
  93.3 0.7 copy.15

commit v5 on v4

--- a/solution.py
+++ b/solution.py
@@ -175,7 +175,7 @@
     return (base, half) if d == 1 else (base + half, n - half)
 
 
-def gather_row(s, p, tag, tab):
+def gather_row(s, p, tag, own, tab):
     first, rest = row_parts(tab.shape[2])
     top = NZ // 2
     mine, other = p.yl, 1 - p.yl
@@ -189,17 +189,18 @@
 
     streams = (("b", mine, rest), ("a", mine, first), ("c", other, first))
 
-    def hop(name, yl, part, h):
+    def begin(key, ds, to):
+        s.send((tag,) + key, own.at[pl.ds(*ds)], blk(mine, 0, ds), to)
+
+    begin(("ya",), first[:2], p.across)
+    for name, yl, part in streams[:2]:
         for d, to in ways:
-            push((name, d, h), blk(yl, d * (1 - h), hop_rows(part, d, h)), to)
-
-    push(("ya",), blk(mine, 0, first[:2]), p.across)
-    for name, yl, part in streams[:2]:
-        hop(name, yl, part, 1)
-    push(("yb", 0), blk(mine, 0, rest[:2]), p.across)
+            begin((name, d, 1), part[:2], to)
+    begin(("yb", 0), rest[:2], p.across)
     yield
     s.wait((tag, "ya"), blk(other, 0, first[:2]), p.across)
-    hop(*streams[2], 1)
+    for d, to in ways:
+        push(("c", d, 1), blk(other, 0, first[:2]), to)
     for h in range(1, top + 1):
         for name, yl, part in streams:
             yield
@@ -280,7 +281,7 @@
 
 
 def col_parts(rows):
-    na = rows * 3 // 8 // 32 * 32
+    na = rows // 2
     return na, rows - na
 
 
@@ -289,6 +290,7 @@
     a_, b_ = pl.ds(0, na), pl.ds(na, nb)
     mine, other, core, sib = p.yh, 1 - p.yh, p.core, 1 - p.core
     ways = ((1, p.right, 0), (-1, p.left, 1))
+    groups = (("o", other, 1), ("m", mine, 0))
 
     def a_cut(n):
         return pl.ds(n * (na // 2), na // 2)
@@ -299,41 +301,49 @@
     def whole(h):
         return cbuf.at[:, p.xat(h)]
 
+    def crossed(h):
+        s.wait((tag, "yb", h), yb.at[h % NX], p.across)
+        add_into(part.at[mine, p.xat(h), core, b_], yb.at[h % NX])
+
     for h in (2, 1, -1, 0):
         s.send((tag, "c", h), part.at[:, p.xat(h), sib], whole(h), p.sibling)
     yield
-    for h in (2, 1, -1):
+    for h in (2, 1, -1, 0):
         s.wait((tag, "c", h), whole(h), p.sibling)
         add_into(part.at[:, p.xat(h), core], whole(h))
+        if h == 2:
+            for name, yh, i in groups:
+                for d, to, n in ways:
+                    s.send((tag, "xa2", name, d), part.at[yh, p.xat(2), core, a_cut(n)], xa2.at[i, a_cut(n)], to)
         s.send((tag, "yb", h), part.at[other, p.xat(h), core, b_], yb.at[h % NX], p.across)
-        if h == 2:
+    for name, yh, i in groups:
+        yield
+        for d, to, n in ways:
+            s.wait((tag, "xa2", name, d), xa2.at[i, a_cut(n)], to)
+            add_into(part.at[yh, p.xat(d), core, a_cut(n)], xa2.at[i, a_cut(n)])
+            s.send((tag, "xa1", name, d), part.at[yh, p.xat(d), core, a_], xa1.at[n, i], to)
+        if name == "o":
+            yield
+            crossed(2)
             for d, to, n in ways:
-                s.send((tag, "xa2", d), part.at[:, p.xat(2), core, a_cut(n)], xa2.at[:, a_cut(n)], to)
-    s.wait((tag, "c", 0), whole(0), p.sibling)
-    add_into(part.at[:, p.x, core], whole(0))
-    s.send((tag, "yb", 0), part.at[other, p.x, core, b_], yb.at[0], p.across)
-    yield
-    for d, to, n in ways:
-        s.wait((tag, "xa2", d), xa2.at[:, a_cut(n)], to)
-        add_into(part.at[:, p.xat(d), core, a_cut(n)], xa2.at[:, a_cut(n)])
-        s.send((tag, "xa1", d), part.at[:, p.xat(d), core, a_], xa1.at[n], to)
-    yield
-    s.wait((tag, "yb", 2), yb.at[2], p.across)
-    add_into(part.at[mine, p.xat(2), core, b_], yb.at[2])
-    for d, to, n in ways:
-        s.send((tag, "xb2", d), part.at[mine, p.xat(2), core, b_cut(n, na)], xb2.at[b_cut(n, 0)], to)
-    yield
-    for d, to, n in ways:
-        s.wait((tag, "yb", d), yb.at[d % NX], p.across)
-        add_into(part.at[mine, p.xat(d), core, b_], yb.at[d % NX])
+                s.send((tag, "xb2", d), part.at[mine, p.xat(2), core, b_cut(n, na)], xb2.at[b_cut(n, 0)], to)
+    yield
+    name, yh, i = groups[0]
+    for d, to, n in ways:
+        s.wait((tag, "xa1", name, d), xa1.at[n, i], to)
+    add_into(part.at[yh, p.x, core, a_], xa1.at[0, i], xa1.at[1, i])
+    s.send((tag, "ya"), part.at[other, p.x, core, a_], ya, p.across)
+    yield
+    for d, to, n in ways:
+        crossed(d)
         s.wait((tag, "xb2", d), xb2.at[b_cut(n, 0)], to)
         add_into(part.at[mine, p.xat(d), core, b_cut(n, na)], xb2.at[b_cut(n, 0)])
         s.send((tag, "xb1", d), part.at[mine, p.xat(d), core, b_], xb1.at[n], to)
     yield
-    for d, to, n in ways:
-        s.wait((tag, "xa1", d), xa1.at[n], to)
-    add_into(part.at[:, p.x, core, a_], xa1.at[0], xa1.at[1])
-    s.send((tag, "ya"), part.at[other, p.x, core, a_], ya, p.across)
+    name, yh, i = groups[1]
+    for d, to, n in ways:
+        s.wait((tag, "xa1", name, d), xa1.at[n, i], to)
+    add_into(part.at[yh, p.x, core, a_], xa1.at[0, i], xa1.at[1, i])
     s.wait((tag, "yb", 0), yb.at[0], p.across)
     yield
     for d, to, n in ways:
@@ -363,53 +373,66 @@
     mine, other, core = p.yh, 1 - p.yh, p.core
     ways = ((1, p.right, 0), (-1, p.left, 1))
 
+    def a_cut(n):
+        return pl.ds(n * (na // 2), na // 2)
+
+    def b_cut(n):
+        return pl.ds(na + n * (nb // 2), nb // 2)
+
     def blk(yh, h, ds):
         return tab.at[yh, p.xat(h), core, ds]
 
-    def pair(h, ds):
-        return tab.at[:, p.xat(h), core, ds]
-
     def push(key, b, to):
         s.send((tag,) + key, b, b, to)
 
     def took(key, b):
         s.wait((tag,) + key, b, p.sibling)
 
+    def share(h, name, ds):
+        push(("c", h, name), tab.at[:, p.xat(h), core, ds], p.sibling)
+
     push(("ya",), blk(mine, 0, a_), p.across)
     for d, to, n in ways:
         push(("b", d), blk(mine, 0, b_), to)
     push(("yb", 0), blk(mine, 0, b_), p.across)
+    for d, to, n in ways:
+        push(("m", d), blk(mine, 0, a_), to)
+    yield
+    for d, to, n in ways:
+        took(("b", d), blk(mine, -d, b_))
+        push(("b2", d), blk(mine, -d, b_cut(n)), to)
+        push(("yb", -d), blk(mine, -d, b_), p.across)
     yield
     took(("ya",), blk(other, 0, a_))
     for d, to, n in ways:
-        push(("a", d), pair(0, a_), to)
-    push(("c", 0, "a"), pair(0, a_), p.sibling)
-    yield
-    for d, to, n in ways:
-        took(("b", d), blk(mine, -d, b_))
-        push(("b2", d), blk(mine, -d, pl.ds(na + n * (nb // 2), nb // 2)), to)
-        push(("yb", -d), blk(mine, -d, b_), p.across)
-    yield
-    for d, to, n in ways:
-        took(("a", d), pair(-d, a_))
-        push(("a2", d), pair(-d, pl.ds(n * (na // 2), na // 2)), to)
-        push(("c", -d, "a"), pair(-d, a_), p.sibling)
+        push(("o", d), blk(other, 0, a_), to)
+    share(0, "a", a_)
+    yield
+    for d, to, n in ways:
+        took(("m", d), blk(mine, -d, a_))
+        push(("m2", d), blk(mine, -d, a_cut(n)), to)
     took(("yb", 0), blk(other, 0, b_))
-    push(("c", 0, "b"), pair(0, b_), p.sibling)
-    yield
-    for d, to, n in ways:
-        took(("b2", d), blk(mine, 2, pl.ds(na + n * (nb // 2), nb // 2)))
+    share(0, "b", b_)
+    yield
+    for d, to, n in ways:
+        took(("b2", d), blk(mine, 2, b_cut(n)))
     push(("yb", 2), blk(mine, 2, b_), p.across)
+    yield
+    for d, to, n in ways:
+        took(("o", d), blk(other, -d, a_))
+        push(("o2", d), blk(other, -d, a_cut(n)), to)
+        share(-d, "a", a_)
     yield
     for d in (1, -1):
         took(("yb", d), blk(other, d, b_))
-        push(("c", d, "b"), pair(d, b_), p.sibling)
-    yield
-    for d, to, n in ways:
-        took(("a2", d), pair(2, pl.ds(n * (na // 2), na // 2)))
-    push(("c", 2, "a"), pair(2, a_), p.sibling)
+        share(d, "b", b_)
+    yield
+    for name, yh in (("m2", mine), ("o2", other)):
+        for d, to, n in ways:
+            took((name, d), blk(yh, 2, a_cut(n)))
+    share(2, "a", a_)
     took(("yb", 2), blk(other, 2, b_))
-    push(("c", 2, "b"), pair(2, b_), p.sibling)
+    share(2, "b", b_)
     yield
     for h in (0, 1, -1, 2):
         for name, ds in (("a", a_), ("b", b_)):
@@ -499,20 +522,20 @@
     for c in loads:
         c.start()
     tiles[slots] = jnp.zeros((edge, edge), tiles.dtype)
+    pl.semaphore_wait(barrier, len(peers))
+
+    s = Sender(send_sem, recv_sem)
+    gather = gather_row(s, q, "gr", x_ref, xtab)
+    next(gather)
     n_tiles = stash.shape[0] * 2 - 2 - slots
     for c in loads[:3]:
         c.wait()
     order_slots(tr[pl.ds(mc, 1)], tc[pl.ds(mc, 1)], cnt[mr, mc], n_tiles, plan)
     to_scalars = pltpu.make_async_copy(plan, splan, sems.at[7])
     to_scalars.start()
-    loads[3].wait()
-    pl.semaphore_wait(barrier, len(peers))
-
-    s = Sender(send_sem, recv_sem)
-    gather = gather_row(s, q, "gr", xtab)
     drain(gather)
     to_scalars.wait()
-    for c in loads[4:]:
+    for c in loads[3:]:
         c.wait()
 
     multiply(False, splan, tiles, xtab.reshape(n_tiles, edge, feats), stash)
@@ -539,14 +562,16 @@
     next(weights)
     for c in before:
         c.wait_send()
-    next(gather)
-    next(gather)
+    for _ in range(2):
+        next(gather)
+    next(weights)
+    for _ in range(4):
+        next(gather)
     next(weights)
     drain(gather)
     next(weights)
 
     multiply(True, splan, tiles, etab.reshape(n_tiles, edge, feats), stash)
-    next(weights)
     for t in range(n_tiles):
         b = t // per
         back[b // NZ, b % NZ, pl.ds(t % per * edge, edge)] = stash[splan[7, t]]
@@ -555,7 +580,7 @@
     next(reduce)
     for c in before:
         c.wait_send()
-    for _ in range(3):
+    for _ in range(7):
         next(reduce)
     next(weights)
     for _ in range(5):
@@ -610,8 +635,8 @@
         + reduce_col_scratch(n_yh, NX, rows, feats)
         + reduce_row_scratch(rows, feats)
         + [
-            pltpu.SemaphoreType.DMA((200,)),
-            pltpu.SemaphoreType.DMA((200,)),
+            pltpu.SemaphoreType.DMA((256,)),
+            pltpu.SemaphoreType.DMA((256,)),
             pltpu.SemaphoreType.DMA((8,)),
         ],
         compiler_params=pltpu.CompilerParams(

time: 94.2 us -> 91.3 us (0.969)
  Pallas kernels: 91.3 us -> 88.5 us
    pallas_call x1, Pallas kernels: 91.3 us -> 88.5 us  [layer(): pl.pallas_call(functools.partial(layer_kernel, 1.0 / math.sqrt(rows * n_r...]
where the time goes in v5:
time: 91.3 us; the launch traced here: 91.2 us
  Pallas kernels  88.5 us (97%)
  local copies, waits for them, and re-layouts  2.01 us (2%)
    pallas_call x1, Pallas kernels, layer(): pl.pallas_call(functools.partial(layer_kernel, 1.0 / math.sqrt(rows * n_r...  88.5 us
    unnamed x3, local copies, waits for them, and re-layouts  2.01 us

profile of v5, /device:TPU:1, one launch (start us, length us, event | category | flops | bytes accessed | tf_op | source)
XLA Modules:
  0.0 91.2 jit_solution(7303892034059338382)
XLA Ops:
  0.6 88.5 %layer.1 = (bf16[256,256]{1,0:T(8,128)(2,1)S(1)}, bf16[256,256]{1,0:T(8,128)(2,1)S(1)}, f32[2,4,2,16,256]{4,3,2,1,0:T(8,128)S(1)}) custom-call(bf16[256,256]{1,0:T(8,128)(2,1)} %bitcast.10, bf16[192,128,128]{2,1,0:T(8,128)(2,1)} %bitcast.9, s32[16,16,192]{2,1,0:T(8,128)} %tr_ref.1, s32[16,16,192]{2,1,0:T(8,128)} %tc_ref.1, s32[16,16]{1,0:T(8,128)} %cnt_ref.1, ...), custom_call_target="tpu_custom_call" | custom-call | tf_op jit(solution)/shard_map/layer/pallas_call | solution.py:606
  89.2 0.7 copy.13
  89.8 0.7 copy.14
  90.5 0.7 copy.15

commit v6 on v5

--- a/solution.py
+++ b/solution.py
@@ -66,6 +66,19 @@
 
     def zat(self, hops):
         return lax.rem(self.z + hops + NZ, NZ)
+
+    ORDER = (4, 5, 3, 6, 2, 7, 1, 0)
+
+    def place(self, tile, per):
+        block = tile // per
+        hops = (block % NZ - self.z + NZ) % NZ
+        rank = jnp.zeros_like(tile)
+        for n, h in enumerate(self.ORDER):
+            rank = jnp.where(hops == h, n, rank)
+        return (rank * 2 + block // NZ) * per + tile % per
+
+    def spot(self, place, per):
+        return place // per % 2, self.zat(self.ORDER[place // (2 * per)]), place % per
 
     def at(self, yl, hops):
         return yl * NZ + self.zat(hops)
@@ -89,11 +102,27 @@
     def xat(self, hops):
         return lax.rem(self.x + hops + NX, NX)
 
+    ORDER = (2, 1, 3, 0)
+
+    def place(self, tile, per):
+        block = tile // per
+        hops = (block // 2 % NX - self.x + NX) % NX
+        rank = jnp.zeros_like(tile)
+        for n, h in enumerate(self.ORDER):
+            rank = jnp.where(hops == h, n, rank)
+        rank = rank + jnp.where(block % 2 == self.core, NX, 0)
+        return (rank * 2 + block // (2 * NX)) * per + tile % per
+
+    def spot(self, place, per):
+        rank = place // (2 * per)
+        core = self.core if rank >= NX else 1 - self.core
+        return place // per % 2, self.xat(self.ORDER[rank % NX]), core, place % per
+
     def at(self, yh, hops, core):
         return (yh * NX + self.xat(hops)) * 2 + core
 
 
-def order_slots(rows, cols, live, n_tiles, plan):
+def order_slots(rows, row_place, cols, col_place, live, n_tiles, plan):
     slots = rows.shape[1]
     places = plan.shape[1]
     steps = (slots + n_tiles) // 2
@@ -110,7 +139,7 @@
         return jnp.sum(jnp.where(sub == lane, row, 0), axis=1, keepdims=True)
 
     out = []
-    for key, source in ((rows, cols), (cols, rows)):
+    for key, source in ((row_place, cols), (col_place, rows)):
         same = (turn(key) == key) & (sub < lane) & live_col
         rank = jnp.sum(jnp.where(same, 1, 0), axis=0, keepdims=True)
         number = jnp.sum(jnp.where((tile == key) & live_row, 1, 0), axis=1, keepdims=True)
@@ -129,30 +158,41 @@
         plan[pl.ds(n, 1)] = x
 
 
-GROUP = 28
-
-
-def multiply(flip, plan, tiles, tab, stash):
+EARLY = 4
+LOOPS = 2
+
+
+def multiply(flip, plan, tiles, tab, stash, put):
     steps = stash.shape[0] - 1
+    early = EARLY * tab.shape[0] // 2
     first = 4 if flip else 0
     side = 0 if flip else 1
     shape = stash.shape[1:]
 
-    def some(g, acc):
-        for u in range(GROUP):
-            p = g * GROUP + u
-            k = [plan[first, 2 * p + i] for i in (0, 1)]
-            q = [plan[first + 1, 2 * p + i] for i in (0, 1)]
-            left = jnp.concatenate([tiles[i] for i in k], axis=side)
-            right = jnp.concatenate([tab[i] for i in q], axis=0)
-            prod = lax.dot_general(left, right, (((side,), (0,)), ((), ())), preferred_element_type=F32)
-            fresh = plan[first + 2, 2 * p] == 1
-            acc = jnp.where(fresh, 0.0, acc) + prod
-            stash[p] = acc.astype(stash.dtype)
-        return acc
-
-    lax.fori_loop(0, steps // GROUP, some, jnp.zeros(shape, F32))
+    def run_steps(start, number, acc):
+        def some(g, acc):
+            for u in range(number // LOOPS):
+                p = start + g * (number // LOOPS) + u
+                k = [plan[first, 2 * p + i] for i in (0, 1)]
+                q = [plan[first + 1, 2 * p + i] for i in (0, 1)]
+                left = jnp.concatenate([tiles[i] for i in k], axis=side)
+                right = jnp.concatenate([tab[i] for i in q], axis=0)
+                prod = lax.dot_general(left, right, (((side,), (0,)), ((), ())), preferred_element_type=F32)
+                fresh = plan[first + 2, 2 * p] == 1
+                acc = jnp.where(fresh, 0.0, acc) + prod
+                stash[p] = acc.astype(stash.dtype)
+            return acc
+
+        return lax.fori_loop(0, LOOPS, some, acc)
+
     stash[steps] = jnp.zeros(shape, stash.dtype)
+    acc = run_steps(0, early, jnp.zeros(shape, F32))
+    for t in range(EARLY):
+        put(t, stash[plan[first + 3, t]])
+    yield
+    run_steps(early, steps - early, acc)
+    for t in range(EARLY, tab.shape[0]):
+        put(t, stash[plan[first + 3, t]])
 
 
 def add_into(dst, *terms):
@@ -237,6 +277,7 @@
     for st in streams[:2]:
         for w in ways:
             hop(*st, *w, top)
+    yield
     for h in [d * h for h in range(top - 1, 0, -1) for d in (1, -1)] + [0]:
         s.send((tag, "yb", h), blk(other, h, rest[:2]), ybuf.at[h + top - 1], p.across)
     yield
@@ -307,6 +348,8 @@
 
     for h in (2, 1, -1, 0):
         s.send((tag, "c", h), part.at[:, p.xat(h), sib], whole(h), p.sibling)
+        if h == 2:
+            yield
     yield
     for h in (2, 1, -1, 0):
         s.wait((tag, "c", h), whole(h), p.sibling)
@@ -485,14 +528,6 @@
         pass
 
 
-def drain_after(s, steps):
-    before, s.sent = s.sent, []
-    next(steps)
-    for c in before:
-        c.wait_send()
-    drain(steps)
-
-
 def layer_kernel(
     scale, x_ref, tiles_ref, tr_ref, tc_ref, cnt_ref, w_ref, g_ref, act_ref, grad_ref, wg_ref,
     xtab, etab, tiles, stash, part, back, plan, splan, tr, tc, cnt, w, g, wpart, wc, wd, wy, wz, *rest,
@@ -530,7 +565,8 @@
     n_tiles = stash.shape[0] * 2 - 2 - slots
     for c in loads[:3]:
         c.wait()
-    order_slots(tr[pl.ds(mc, 1)], tc[pl.ds(mc, 1)], cnt[mr, mc], n_tiles, plan)
+    t_rows, t_cols = tr[pl.ds(mc, 1)], tc[pl.ds(mc, 1)]
+    order_slots(t_rows, p.place(t_rows, per), t_cols, q.place(t_cols, per), cnt[mr, mc], n_tiles, plan)
     to_scalars = pltpu.make_async_copy(plan, splan, sems.at[7])
     to_scalars.start()
     drain(gather)
@@ -538,12 +574,20 @@
     for c in loads[3:]:
         c.wait()
 
-    multiply(False, splan, tiles, xtab.reshape(n_tiles, edge, feats), stash)
-    for t in range(n_tiles):
-        b = t // per
-        part[b // (2 * NX), b // 2 % NX, b % 2, pl.ds(t % per * edge, edge)] = stash[splan[3, t]]
+    def put_part(place, value):
+        yh, x, core, n = p.spot(place, per)
+        part[yh, x, core, pl.ds(n * edge, edge)] = value
+
+    product = multiply(False, splan, tiles, xtab.reshape(n_tiles, edge, feats), stash, put_part)
+    next(product)
     reduce = reduce_col(s, p, "rc", part, *for_col)
-    drain_after(s, reduce)
+    before, s.sent = s.sent, []
+    next(reduce)
+    drain(product)
+    next(reduce)
+    for c in before:
+        c.wait_send()
+    drain(reduce)
 
     agg = part[p.yh, p.x, p.core]
     pre = jnp.dot(agg, w[...], preferred_element_type=F32)
@@ -562,22 +606,24 @@
     next(weights)
     for c in before:
         c.wait_send()
-    for _ in range(2):
-        next(gather)
-    next(weights)
-    for _ in range(4):
+    for _ in range(3):
         next(gather)
     next(weights)
     drain(gather)
     next(weights)
 
-    multiply(True, splan, tiles, etab.reshape(n_tiles, edge, feats), stash)
-    for t in range(n_tiles):
-        b = t // per
-        back[b // NZ, b % NZ, pl.ds(t % per * edge, edge)] = stash[splan[7, t]]
+    def put_back(place, value):
+        yl, z, n = q.spot(place, per)
+        back[yl, z, pl.ds(n * edge, edge)] = value
+
+    product = multiply(True, splan, tiles, etab.reshape(n_tiles, edge, feats), stash, put_back)
+    next(product)
     before, s.sent = s.sent, []
     reduce = reduce_row(s, q, "rr", back, *for_row)
     next(reduce)
+    drain(product)
+    next(reduce)
+    next(weights)
     for c in before:
         c.wait_send()
     for _ in range(7):

time: 91.3 us -> 87.9 us (0.963)
  Pallas kernels: 88.5 us -> 85.1 us
    pallas_call x1, Pallas kernels: 88.5 us -> 85.1 us  [layer(): pl.pallas_call(functools.partial(layer_kernel, 1.0 / math.sqrt(rows * n_r...]
where the time goes in v6:
time: 87.9 us; the launch traced here: 87.8 us
  Pallas kernels  85.1 us (97%)
  local copies, waits for them, and re-layouts  2.01 us (2%)
    pallas_call x1, Pallas kernels, layer(): pl.pallas_call(functools.partial(layer_kernel, 1.0 / math.sqrt(rows * n_r...  85.1 us
    unnamed x3, local copies, waits for them, and re-layouts  2.01 us

profile of v6, /device:TPU:1, one launch (start us, length us, event | category | flops | bytes accessed | tf_op | source)
XLA Modules:
  0.0 87.8 jit_solution(14390775756294784964)
XLA Ops:
  0.6 85.1 %layer.1 = (bf16[256,256]{1,0:T(8,128)(2,1)S(1)}, bf16[256,256]{1,0:T(8,128)(2,1)S(1)}, f32[2,4,2,16,256]{4,3,2,1,0:T(8,128)S(1)}) custom-call(bf16[256,256]{1,0:T(8,128)(2,1)} %bitcast.10, bf16[192,128,128]{2,1,0:T(8,128)(2,1)} %bitcast.9, s32[16,16,192]{2,1,0:T(8,128)} %tr_ref.1, s32[16,16,192]{2,1,0:T(8,128)} %tc_ref.1, s32[16,16]{1,0:T(8,128)} %cnt_ref.1, ...), custom_call_target="tpu_custom_call" | custom-call | tf_op jit(solution)/shard_map/layer/pallas_call | solution.py:652
  85.8 0.7 copy.13
  86.4 0.7 copy.14
  87.1 0.7 copy.15

commit v7 on v6

--- a/solution.py
+++ b/solution.py
@@ -437,9 +437,9 @@
     push(("ya",), blk(mine, 0, a_), p.across)
     for d, to, n in ways:
         push(("b", d), blk(mine, 0, b_), to)
+    for d, to, n in ways:
+        push(("m", d), blk(mine, 0, a_), to)
     push(("yb", 0), blk(mine, 0, b_), p.across)
-    for d, to, n in ways:
-        push(("m", d), blk(mine, 0, a_), to)
     yield
     for d, to, n in ways:
         took(("b", d), blk(mine, -d, b_))
@@ -529,7 +529,7 @@
 
 
 def layer_kernel(
-    scale, x_ref, tiles_ref, tr_ref, tc_ref, cnt_ref, w_ref, g_ref, act_ref, grad_ref, wg_ref,
+    scale, x_ref, tiles_ref, tr_ref, tc_ref, cnt_ref, w_ref, g_ref, out_ref, wg_ref,
     xtab, etab, tiles, stash, part, back, plan, splan, tr, tc, cnt, w, g, wpart, wc, wd, wy, wz, *rest,
 ):
     n_col, n_row = 7, 5
@@ -599,7 +599,7 @@
     before, s.sent = s.sent, []
     gather = gather_col(s, p, "gc", etab)
     next(gather)
-    act_ref[...] = (pre * logistic).astype(BF16)
+    out_ref[0] = (pre * logistic).astype(BF16)
     wg = lax.dot_general(agg, d_pre, (((0,), (0,)), ((), ())), preferred_element_type=F32)
     wpart[...] = wg.reshape(wpart.shape)
     weights = sum_weight(s, p, q, wpart, wc, wd, wy, wz, wg_ref, scale)
@@ -633,7 +633,7 @@
         next(reduce)
     next(weights)
     drain(reduce)
-    grad_ref[...] = back[q.yl, q.z]
+    out_ref[1] = back[q.yl, q.z]
     drain(weights)
     s.finish()
 
@@ -652,12 +652,11 @@
     return pl.pallas_call(
         functools.partial(layer_kernel, 1.0 / math.sqrt(rows * n_row * n_col)),
         out_shape=(
-            vmem((rows, feats), BF16),
-            vmem((rows, feats), BF16),
+            vmem((2, rows, feats), BF16),
             vmem((n_yh, NX, 2, n_w, feats), F32),
         ),
         in_specs=[hbm] * 7,
-        out_specs=[pl.BlockSpec(memory_space=vmem)] * 3,
+        out_specs=[pl.BlockSpec(memory_space=vmem)] * 2,
         scratch_shapes=[
             vmem((n_row // NZ, NZ, rows, feats), BF16),
             vmem((n_yh, NX, 2, rows, feats), BF16),
@@ -693,10 +692,10 @@
 
 
 def per_device(node_features, tile_values, tile_rows, tile_cols, tile_count, weight, cotangent):
-    act, grad, wgrad = layer(
+    results, wgrad = layer(
         node_features[0, 0], tile_values[0, 0], tile_rows, tile_cols, tile_count, weight, cotangent[0, 0]
     )
-    return act[None, None], grad[None, None], wgrad.reshape(weight.shape)
+    return results[:1, None], results[1:, None], wgrad.reshape(weight.shape)
 
 
 def solution(mesh):

time: 87.9 us -> 87.3 us (level)
    unnamed x3 -> x1, local copies, waits for them, and re-layouts: 2.01 us -> 0.71 us
where the time goes in v7:
time: 87.3 us; the launch traced here: 87.2 us
  Pallas kernels  85.2 us (98%)
  local copies, waits for them, and re-layouts  1.42 us (2%)
    pallas_call x1, Pallas kernels, layer(): pl.pallas_call(functools.partial(layer_kernel, 1.0 / math.sqrt(rows * n_r...  85.2 us

profile of v7, /device:TPU:1, one launch (start us, length us, event | category | flops | bytes accessed | tf_op | source)
XLA Modules:
  0.0 87.2 jit_solution(2369307055251100151)
XLA Ops:
  0.6 85.2 %layer.1 = (bf16[2,256,256]{2,1,0:T(8,128)(2,1)S(1)}, f32[2,4,2,16,256]{4,3,2,1,0:T(8,128)S(1)}) custom-call(bf16[256,256]{1,0:T(8,128)(2,1)} %bitcast.10, bf16[192,128,128]{2,1,0:T(8,128)(2,1)} %bitcast.9, s32[16,16,192]{2,1,0:T(8,128)} %tr_ref.1, s32[16,16,192]{2,1,0:T(8,128)} %tc_ref.1, s32[16,16]{1,0:T(8,128)} %cnt_ref.1, bf16[256,256]{1,0:T(8,128)(2,1)} %w_ref.1, ...), custom_call_target="tpu_custom_call" | custom-call | tf_op jit(solution)/shard_map/layer/pallas_call | solution.py:652
  85.8 0.7 copy.11
  86.5 0.7 slice_bitcast_fusion

commit v8 on v7

--- a/solution.py
+++ b/solution.py
@@ -67,7 +67,7 @@
     def zat(self, hops):
         return lax.rem(self.z + hops + NZ, NZ)
 
-    ORDER = (4, 5, 3, 6, 2, 7, 1, 0)
+    ORDER = (4, 3, 5, 2, 6, 1, 7, 0)
 
     def place(self, tile, per):
         block = tile // per
@@ -193,6 +193,8 @@
     run_steps(early, steps - early, acc)
     for t in range(EARLY, tab.shape[0]):
         put(t, stash[plan[first + 3, t]])
+        if (t + 1) % EARLY == 0:
+            yield
 
 
 def add_into(dst, *terms):
@@ -280,7 +282,7 @@
     yield
     for h in [d * h for h in range(top - 1, 0, -1) for d in (1, -1)] + [0]:
         s.send((tag, "yb", h), blk(other, h, rest[:2]), ybuf.at[h + top - 1], p.across)
-    yield
+        yield
     crossed(top)
     for w in ways:
         hop(*streams[2], *w, top)
@@ -348,9 +350,7 @@
 
     for h in (2, 1, -1, 0):
         s.send((tag, "c", h), part.at[:, p.xat(h), sib], whole(h), p.sibling)
-        if h == 2:
-            yield
-    yield
+        yield
     for h in (2, 1, -1, 0):
         s.wait((tag, "c", h), whole(h), p.sibling)
         add_into(part.at[:, p.xat(h), core], whole(h))
@@ -582,9 +582,11 @@
     next(product)
     reduce = reduce_col(s, p, "rc", part, *for_col)
     before, s.sent = s.sent, []
+    for _ in range(NX - 1):
+        next(reduce)
+        next(product)
     next(reduce)
     drain(product)
-    next(reduce)
     for c in before:
         c.wait_send()
     drain(reduce)
@@ -620,9 +622,11 @@
     next(product)
     before, s.sent = s.sent, []
     reduce = reduce_row(s, q, "rr", back, *for_row)
+    for _ in range(NZ - 1):
+        next(reduce)
+        next(product)
     next(reduce)
     drain(product)
-    next(reduce)
     next(weights)
     for c in before:
         c.wait_send()

time: 87.3 us -> 87.7 us (level)
  no operation moved by 1% of the time
where the time goes in v8:
time: 87.7 us; the launch traced here: 87.6 us
  Pallas kernels  85.5 us (97%)
  local copies, waits for them, and re-layouts  1.42 us (2%)
    pallas_call x1, Pallas kernels, layer(): pl.pallas_call(functools.partial(layer_kernel, 1.0 / math.sqrt(rows * n_r...  85.5 us

profile of v8, /device:TPU:1, one launch (start us, length us, event | category | flops | bytes accessed | tf_op | source)
XLA Modules:
  0.0 87.6 jit_solution(409755050395676098)
XLA Ops:
  0.6 85.5 %layer.1 = (bf16[2,256,256]{2,1,0:T(8,128)(2,1)S(1)}, f32[2,4,2,16,256]{4,3,2,1,0:T(8,128)S(1)}) custom-call(bf16[256,256]{1,0:T(8,128)(2,1)} %bitcast.10, bf16[192,128,128]{2,1,0:T(8,128)(2,1)} %bitcast.9, s32[16,16,192]{2,1,0:T(8,128)} %tr_ref.1, s32[16,16,192]{2,1,0:T(8,128)} %tc_ref.1, s32[16,16]{1,0:T(8,128)} %cnt_ref.1, bf16[256,256]{1,0:T(8,128)(2,1)} %w_ref.1, ...), custom_call_target="tpu_custom_call" | custom-call | tf_op jit(solution)/shard_map/layer/pallas_call | solution.py:656
  86.2 0.7 copy.11
  86.9 0.7 slice_bitcast_fusion
